TPU v7x, 32 devices: a whole 2x2x4 slice. The times are simulated.
32 devices in a mesh: groups: 2 (over x), gx: 8 (over z, y), gy: 2 (over core).
Axes of the slice: x: 2, y: 2, z: 4, core: 2. Of those that a mesh axis runs over, the one named last changes fastest.
Arguments:
- states: bfloat16 [2048, 16384], P('groups', ('gy', 'gx')), parts along dimension 0
- norm_gain: bfloat16 [16384], P(('gy', 'gx')), may hold values from 0.099609375 to 1.8984375
- w_query: bfloat16 [16384, 8192], P('gy', 'gx'), may hold values from -0.046875 to 0.046875
- keyvalue_weight: bfloat16 [16384, 1024], P('gy', 'gx'), may hold values from -0.046875 to 0.046875
- w_output: bfloat16 [8192, 2, 8, 1024], P('gx', 'gy'), may hold values from -0.25 to 0.25
- key_cache: bfloat16 [2048, 4, 64, 128], P(('groups', 'gy', 'gx')), parts along dimension 0
- cached_value_rows: bfloat16 [2048, 4, 64, 128], P(('groups', 'gy', 'gx')), parts along dimension 0, may hold values from -6 to 6
- lengths: int32 [2048], P(('groups', 'gy', 'gx')), parts along dimension 0, may hold values from 1 to 64, as said below
Outputs:
- layer_out: bfloat16 [2048, 16384], P('groups', ('gy', 'gx')), parts along dimension 0
There are 2 independent parts, one for each index of `groups`. A program takes and returns all parts, laid end to end along the dimension named above; an argument that names none is the same for every part. Nothing has to cross between parts.
Inputs may be any that keep to these rules, and one draw needn't show every extreme that they name: `lengths`: the largest, 64, is reached in every draw.
All inputs are finite; a program needn't handle non-finite values.
Results may differ from a plain program's by a relative error of at most 0.017.
Values may be sent and summed in bfloat16 or wider, within the bound.
A program may use at most 192 MiB of HBM per device.

v0:
```python
import math

import jax
import jax.numpy as jnp
from jax import lax
from jax.sharding import PartitionSpec as P

MODEL_WIDTH = 16384


epsilon = 1e-05
rope_base = 500000.0


def rotate(vectors, positions):
    middle = vectors.shape[-1] // 2
    frequency = rope_base ** (-jnp.arange(middle, dtype=jnp.float32) * 2.0 / vectors.shape[-1])
    angles = positions.astype(jnp.float32)[:, None] * frequency[None, :]
    cosine = jnp.cos(angles)[:, None, :]
    sine_part = jnp.sin(angles)[:, None, :]
    leading = vectors[..., :middle]
    trailing = vectors[..., middle:]
    return jnp.concatenate(
        [leading * cosine - trailing * sine_part, trailing * cosine + leading * sine_part], axis=-1
    )


def attend(queries, new_keys, new_values, key_cache, cached_value_rows, lengths):
    row_count, kv_heads, context, head_dim = key_cache.shape
    heads = queries.shape[1] // head_dim
    per_group = heads // kv_heads
    query_rot = rotate(
        queries.astype(jnp.float32).reshape(row_count, heads, head_dim), lengths
    ).astype(jnp.bfloat16)
    key_rot = rotate(
        new_keys.astype(jnp.float32).reshape(row_count, kv_heads, head_dim), lengths
    ).astype(jnp.bfloat16)
    query_grp = query_rot.reshape(row_count, kv_heads, per_group, head_dim)
    scaling = 1.0 / math.sqrt(head_dim)
    cached = (
        jnp.einsum("rgjd,rgcd->rgjc", query_grp, key_cache, preferred_element_type=jnp.float32)
        * scaling
    )
    own_score = (
        jnp.einsum("rgjd,rgd->rgj", query_grp, key_rot, preferred_element_type=jnp.float32)
        * scaling
    )
    is_live = (jnp.arange(context)[None, :] < lengths[:, None])[:, None, None, :]
    cached = jnp.where(is_live, cached, -jnp.inf)
    peak_score = jnp.maximum(jnp.max(cached, axis=-1), own_score)
    weights = jnp.where(is_live, jnp.exp(cached - peak_score[..., None]), 0.0)
    own_weight = jnp.exp(own_score - peak_score)
    total = jnp.sum(weights, axis=-1) + own_weight
    own_prob = lax.optimization_barrier(own_weight.astype(jnp.bfloat16)).astype(jnp.float32)
    mixed = jnp.einsum(
        "rgjc,rgcd->rgjd",
        weights.astype(jnp.bfloat16),
        cached_value_rows,
        preferred_element_type=jnp.float32,
    )
    mixed = mixed + own_prob[..., None] * new_values.astype(jnp.float32).reshape(
        row_count, kv_heads, 1, head_dim
    )
    return (mixed / total[..., None]).astype(jnp.bfloat16).reshape(row_count, heads * head_dim)


def shards(
    states, norm_gain, w_query, keyvalue_weight, w_output, key_cache, cached_value_rows, lengths
):
    whole_states, whole_gain = (
        lax.all_gather(states, "gx", axis=1, tiled=True),
        lax.all_gather(norm_gain, "gx", axis=0, tiled=True),
    )
    states_f = whole_states.astype(jnp.float32)
    squares = lax.psum(jnp.sum(states_f * states_f, axis=1), "gy")
    norm_scale = lax.rsqrt(squares / MODEL_WIDTH + epsilon)
    normed = (states_f * norm_scale[:, None] * whole_gain.astype(jnp.float32)[None, :]).astype(
        jnp.bfloat16
    )
    query_part = jnp.dot(normed, w_query, preferred_element_type=jnp.float32)
    keyval_part = jnp.dot(normed, keyvalue_weight, preferred_element_type=jnp.float32)
    query_sum, keyval_sum = (
        lax.psum_scatter(
            query_part.astype(jnp.bfloat16), "gy", scatter_dimension=0, tiled=True
        ).astype(jnp.float32),
        lax.psum_scatter(
            keyval_part.astype(jnp.bfloat16), "gy", scatter_dimension=0, tiled=True
        ).astype(jnp.float32),
    )
    queries, keyvals = (
        lax.all_to_all(
            query_sum.astype(jnp.bfloat16), "gx", split_axis=0, concat_axis=1, tiled=True
        ),
        lax.all_to_all(
            keyval_sum.astype(jnp.bfloat16), "gx", split_axis=0, concat_axis=1, tiled=True
        ),
    )
    key_span_width = keyvals.shape[1] // 2
    attended = attend(
        queries,
        keyvals[:, :key_span_width],
        keyvals[:, key_span_width:],
        key_cache,
        cached_value_rows,
        lengths,
    )
    head_rows = lax.all_to_all(attended, "gx", split_axis=1, concat_axis=0, tiled=True)
    gathered = lax.all_gather(head_rows, "gy", axis=0, tiled=True)
    out_block = w_output.shape[3]
    output_cols = w_output.reshape(w_output.shape[0], -1)
    partial_value = jnp.dot(gathered, output_cols, preferred_element_type=jnp.float32)
    summed = lax.psum_scatter(
        partial_value.reshape(partial_value.shape[0], 1 * lax.axis_size("gx"), out_block)
        .transpose(1, 0, 2)
        .astype(jnp.bfloat16),
        "gx",
        scatter_dimension=0,
        tiled=True,
    ).astype(jnp.float32)
    return (states.astype(jnp.float32) + summed[0]).astype(jnp.bfloat16)


def solution(mesh):
    return jax.shard_map(
        shards,
        mesh=mesh,
        in_specs=(
            P("groups", ("gy", "gx")),
            P(("gy", "gx")),
            P("gy", "gx"),
            P("gy", "gx"),
            P("gx", "gy", None, None),
            P(("groups", "gy", "gx"), None, None, None),
            P(("groups", "gy", "gx"), None, None, None),
            P(("groups", "gy", "gx")),
        ),
        out_specs=P("groups", ("gy", "gx")),
        check_vma=False,
    )
```

profile of v0, /device:TPU:0, one launch (start us, length us, event | category | flops | bytes accessed | tf_op | source)
XLA Modules:
  0.0 725.4 jit_solution(17203566023764855277)
XLA Ops:
  6.5 0.7 all-gather.3.cloned.1.call-update
  7.4 28.1 %all_gather.10 = bf16[8192]{0:T(1024)(128)(2,1)S(1)} all-gather(bf16[1024]{0:T(1024)(128)(2,1)S(1)} %copy-done.3), channel_id=1, replica_groups=mesh['groups'=2,'gx'=8,'gy'=2] {'gx'}, dimensions={0}, use_global_device_ids=true | all-gather | bytes 18432 | tf_op jit(solution)/shard_map/all_gather | solution.py:72
  35.4 204.5 %all-gather.3.cloned.1.call-done = bf16[1024,8192]{1,0:T(8,128)(2,1)} async-done(((bf16[1024,1024]{1,0:T(8,128)(2,1)}), bf16[1024,8192]{1,0:T(8,128)(2,1)}) %all-gather.3.cloned.1.call-update) | async-done | bytes 16777232 | tf_op jit(solution)/shard_map/all_gather | solution.py:71
  240.0 7.2 fusion
  247.2 2.5 psum.7
  249.7 11.0 %fusion.15 = bf16[1024,128]{1,0:T(8,128)(2,1)} fusion(bf16[8192,128]{1,0:T(8,128)(2,1)S(1)} %copy-done, bf16[1024,8192]{1,0:T(8,128)(2,1)} %all-gather.3.cloned.1.call-done, f32[8192]{0:T(1024)S(1)} %convert_element_type.65, f32[1024]{0:T(1024)S(1)} %add_rsqrt_fusion), kind=kOutput, calls=%fused_computation.21 | convolution fusion | flops 2181169152 | bytes 19173376 | tf_op jit(solution)/shard_map/dot_general | solution.py:81
  260.7 23.4 %fusion.9 = bf16[1024,1024]{1,0:T(8,128)(2,1)} fusion(bf16[8192,1024]{1,0:T(8,128)(2,1)} %param.10, bf16[1024,8192]{1,0:T(8,128)(2,1)} %all-gather.3.cloned.1.call-done, f32[8192]{0:T(1024)S(1)} %convert_element_type.65, f32[1024]{0:T(1024)S(1)} %add_rsqrt_fusion), kind=kOutput, calls=%fused_computation.17 | convolution fusion | flops 17214472192 | bytes 35688448 | tf_op jit(solution)/shard_map/dot_general | solution.py:80
  284.2 10.9 %all_to_all.51 = bf16[8,64,128]{2,1,0:T(8,128)(2,1)S(1)} all-to-all(bf16[8,64,128]{2,1,0:T(8,128)(2,1)} %bitcast.51), channel_id=1, replica_groups=mesh['groups'=2,'gx'=8,'gy'=2] {'gx'}, dimensions={0} | all-to-all | bytes 262144 | tf_op jit(solution)/shard_map/all_to_all | solution.py:94
  295.1 3.6 all-to-all-start
  298.7 0.2 all-gather.5.cloned.1.call-start
  299.0 0.2 multiply_cosine_fusion
  299.4 0.2 subtract_convert_fusion.1
  299.6 0.1 maximum_bitcast_fusion
  299.7 24.6 %all-to-all-done = bf16[8,64,1024]{2,1,0:T(8,128)(2,1)S(1)} async-done(((bf16[8,64,1024]{2,1,0:T(8,128)(2,1)}), bf16[8,64,1024]{2,1,0:T(8,128)(2,1)S(1)}, u32[]{:S(2)}, u32[]{:S(2)}) %all-to-all-start) | async-done | bytes 1048608 | tf_op jit(solution)/shard_map/all_to_all | solution.py:91
  324.3 0.2 convert_bitcast_fusion.1
  324.6 2.5 copy.15
  327.1 1.7 reshape.109
  328.8 0.8 subtract_convert_fusion
  329.7 0.7 fusion.24
  330.4 0.6 copy-done.2
  331.0 2.6 fusion.12
  333.7 1.4 fusion.13
  335.2 2.1 divide_convert_fusion
  337.3 0.5 all_to_all.44
  337.8 0.6 copy.17
  338.4 29.3 %all_to_all.52 = bf16[64,8,1024]{2,0,1:T(8,128)(2,1)} all-to-all(bf16[64,8,1024]{2,0,1:T(8,128)(2,1)S(1)} %copy.17), channel_id=1, replica_groups=mesh['groups'=2,'gx'=8,'gy'=2] {'gx'}, dimensions={1} | all-to-all | bytes 2097152 | tf_op jit(solution)/shard_map/all_to_all | solution.py:107
  367.7 0.3 reduce-scatter.8.cloned.1.call-start
  368.0 18.8 %copy.22 = bf16[128,8,8,1024]{3,1,2,0:T(8,128)(2,1)} copy(bf16[128,8,8,1024]{3,2,1,0:T(8,128)(2,1)} %bitcast.41) | data formatting | bytes 33554432
  386.8 22.4 %copy.18 = bf16[8192,1024]{1,0:T(8,128)(2,1)} copy(bf16[8192,1024]{0,1:T(8,128)(2,1)} %bitcast.40) | data formatting | bytes 33554432 | tf_op jit(solution)/shard_map/dot_general | solution.py:111
  409.2 23.2 %convert_bitcast_fusion = bf16[8,1024,1024]{2,1,0:T(8,128)(2,1)} fusion(bf16[8,1024,1024]{2,1,0:T(8,128)(2,1)} %bitcast.42, bf16[1024,1024]{1,0:T(8,128)(2,1)} %all-gather.5.cloned.1.call-done), kind=kOutput, calls=%fused_computation.5 | convolution fusion | flops 17188257792 | bytes 35651584 | tf_op jit(solution)/shard_map/dot_general | solution.py:111
  432.4 282.0 %reduce-scatter.8.cloned.1.call-done = bf16[1,1024,1024]{2,1,0:T(8,128)(2,1)} async-done(((bf16[8,1024,1024]{2,1,0:T(8,128)(2,1)}), bf16[1,1024,1024]{2,1,0:T(8,128)(2,1)}) %reduce-scatter.8.cloned.1.call-update) | async-done | bytes 2097168 | tf_op jit(solution)/shard_map/reduce_scatter | solution.py:112
  714.4 4.5 fusion.7
  (33 shorter events, 0.7 us)
Async XLA Ops:
  6.5 243.1 %copy-start = (bf16[8192,128]{1,0:T(8,128)(2,1)S(1)}, bf16[8192,128]{1,0:T(8,128)(2,1)}, u32[]{:S(2)}) copy-start(bf16[8192,128]{1,0:T(8,128)(2,1)} %param.11) | copy-start | bytes 6291460
  6.5 0.8 copy-start.3
  6.5 233.4 %all-gather.3.cloned.1.call-start = ((), (), s32[]{:S(2)}) async-start(), calls=%async_computation.6 | async-start | bytes 18874368 | tf_op jit(solution)/shard_map/all_gather | solution.py:71
  7.3 277.0 %reduce-scatter.6.cloned.1.call-start = ((), (), s32[]{:S(2)}) async-start(), calls=%async_computation.8 | async-start | bytes 393216 | tf_op jit(solution)/shard_map/reduce_scatter | solution.py:86
  260.7 34.4 %reduce-scatter.4.cloned.1.call-start = ((), (), s32[]{:S(2)}) async-start(), calls=%async_computation.7 | async-start | bytes 3145728 | tf_op jit(solution)/shard_map/reduce_scatter | solution.py:83
  284.2 14.7 %copy-start.4 = (s32[64]{0:T(128)S(1)}, s32[64]{0:T(128)}, u32[]{:S(2)}) copy-start(s32[64]{0:T(128)} %param.15) | copy-start | bytes 772
  295.1 29.2 %all-to-all-start = ((bf16[8,64,1024]{2,1,0:T(8,128)(2,1)}), bf16[8,64,1024]{2,1,0:T(8,128)(2,1)S(1)}, u32[]{:S(2)}, u32[]{:S(2)}) async-start(bf16[8,64,1024]{2,1,0:T(8,128)(2,1)} %bitcast.48), calls=%async_computation.1 | async-start | bytes 2097152 | tf_op jit(solution)/shard_map/all_to_all | solution.py:91
  298.7 110.5 %all-gather.5.cloned.1.call-start = ((), (), s32[]{:S(2)}) async-start(), calls=%async_computation.9 | async-start | bytes 3145728 | tf_op jit(solution)/shard_map/all_gather | solution.py:108
  328.8 2.2 copy-start.2
  331.0 4.2 copy-start.5
  367.7 346.7 %reduce-scatter.8.cloned.1.call-start = ((), (), s32[]{:S(2)}) async-start(), calls=%async_computation.10 | async-start | bytes 18874368 | tf_op jit(solution)/shard_map/reduce_scatter | solution.py:112
  432.4 286.5 %copy-start.1 = (bf16[8192,128]{1,0:T(8,128)(2,1)S(1)}, bf16[8192,128]{1,0:T(8,128)(2,1)}, u32[]{:S(2)}) copy-start(bf16[8192,128]{1,0:T(8,128)(2,1)} %param.11) | copy-start | bytes 6291460
Sparse Core Ops, SparseCore 0:
  9.5 230.3 all-gather.2
  260.8 5.8 reduce-scatter.5
  284.3 7.8 reduce-scatter.3
  367.8 9.5 all-gather.4
  432.5 281.8 reduce-scatter.7
where the time goes:
time: 727 us; the launch traced here: 725 us
  waiting for transfers between devices  512 us (70%)
  blocking collectives  70.7 us (10%)
  matrix products  63.1 us (9%)
  local copies, waits for them, and re-layouts  47.3 us (7%)
  other arithmetic  14.9 us (2%)
  between operations  13.3 us (2%)
    reduce_scatter x1, waiting for transfers between devices, shards(): lax.psum_scatter(partial_value.reshape(partial_value.shape[0], 1 * lax.ax...  282 us
    all_gather x1, waiting for transfers between devices, shards(): lax.all_gather(states, 'gx', axis=1, tiled=True)  205 us
    all_to_all x1, blocking collectives, shards(): lax.all_to_all(attended, 'gx', split_axis=1, concat_axis=0, tiled=True)  29.3 us
    all_gather x1, blocking collectives, shards(): lax.all_gather(norm_gain, 'gx', axis=0, tiled=True)  28.1 us
    all_to_all x1, waiting for transfers between devices, shards(): lax.all_to_all(query_sum.astype(jnp.bfloat16), 'gx', split_axis=0, concat...  24.6 us
    dot_general x1, matrix products, shards(): query_part = jnp.dot(normed, w_query, preferred_element_type=jnp.float32)  23.4 us
    dot_general x1, matrix products, shards(): jnp.dot(gathered, output_cols, preferred_element_type=jnp.float32)  23.2 us
    dot_general x1, local copies, waits for them, and re-layouts, shards(): jnp.dot(gathered, output_cols, preferred_element_type=jnp.float32)  22.4 us
  transfers between devices with their start and end apart: 6, of which 3 were waited for; matrix products, arithmetic and copies ran while one was open for 9% of the time, Pallas kernels for 0%

commit v1 on v0

--- a/solution.py
+++ b/solution.py
@@ -64,37 +64,104 @@
     return (mixed / total[..., None]).astype(jnp.bfloat16).reshape(row_count, heads * head_dim)
 
 
+def ring_order(size):
+    if size == 8:
+        return [0, 2, 4, 6, 7, 5, 3, 1]
+    return list(range(size))
+
+
 def shards(
     states, norm_gain, w_query, keyvalue_weight, w_output, key_cache, cached_value_rows, lengths
 ):
-    whole_states, whole_gain = (
-        lax.all_gather(states, "gx", axis=1, tiled=True),
-        lax.all_gather(norm_gain, "gx", axis=0, tiled=True),
-    )
-    states_f = whole_states.astype(jnp.float32)
-    squares = lax.psum(jnp.sum(states_f * states_f, axis=1), "gy")
-    norm_scale = lax.rsqrt(squares / MODEL_WIDTH + epsilon)
-    normed = (states_f * norm_scale[:, None] * whole_gain.astype(jnp.float32)[None, :]).astype(
-        jnp.bfloat16
-    )
-    query_part = jnp.dot(normed, w_query, preferred_element_type=jnp.float32)
-    keyval_part = jnp.dot(normed, keyvalue_weight, preferred_element_type=jnp.float32)
-    query_sum, keyval_sum = (
-        lax.psum_scatter(
-            query_part.astype(jnp.bfloat16), "gy", scatter_dimension=0, tiled=True
-        ).astype(jnp.float32),
-        lax.psum_scatter(
-            keyval_part.astype(jnp.bfloat16), "gy", scatter_dimension=0, tiled=True
-        ).astype(jnp.float32),
-    )
-    queries, keyvals = (
-        lax.all_to_all(
-            query_sum.astype(jnp.bfloat16), "gx", split_axis=0, concat_axis=1, tiled=True
-        ),
-        lax.all_to_all(
-            keyval_sum.astype(jnp.bfloat16), "gx", split_axis=0, concat_axis=1, tiled=True
-        ),
-    )
+    size = lax.axis_size("gx")
+    me = lax.axis_index("gx")
+    core = lax.axis_index("gy")
+    order = ring_order(size)
+    order_arr = jnp.array(order, jnp.int32)
+    place_arr = jnp.array([order.index(i) for i in range(size)], jnp.int32)
+    place = place_arr[me]
+    hops = {1: [(order[i], order[(i + 1) % size]) for i in range(size)],
+            -1: [(order[(i + 1) % size], order[i]) for i in range(size)]}
+    long_way = size // 2
+    reach = {(1, 0): long_way, (-1, 0): size - 1 - long_way,
+             (1, 1): size - 1 - long_way, (-1, 1): long_way}
+    chains = list(reach)
+
+    def at_place(offset):
+        return order_arr[lax.rem(place + offset + size, size)]
+
+    row_count, width = states.shape
+    half_rows = row_count // 2
+    other = 1 - core
+
+    def half_of(array, half):
+        return lax.dynamic_slice_in_dim(
+            array, jnp.where(half == 0, other, core) * half_rows, half_rows, 0
+        )
+
+    state_halves = [half_of(states, 0), half_of(states, 1)]
+
+    states_f = states.astype(jnp.float32)
+    gain_all = jnp.zeros((2 * size * width,), jnp.float32)
+    gain_all = lax.dynamic_update_slice(
+        gain_all, norm_gain.astype(jnp.float32), ((core * size + me) * width,)
+    )
+    both = lax.psum(
+        jnp.concatenate([jnp.sum(states_f * states_f, axis=1), gain_all]), ("gx", "gy")
+    )
+    norm_scale = lax.rsqrt(both[:row_count] / MODEL_WIDTH + epsilon)
+    gain_mine = lax.dynamic_slice_in_dim(both[row_count:], core * size * width, size * width, 0)
+    scale_halves = [half_of(norm_scale, 0), half_of(norm_scale, 1)]
+
+    def project(raw, half, owner):
+        gain = lax.dynamic_slice_in_dim(gain_mine, owner * width, width, 0)
+        normed = (
+            raw.astype(jnp.float32) * scale_halves[half][:, None] * gain[None, :]
+        ).astype(jnp.bfloat16)
+        wq = lax.dynamic_slice_in_dim(w_query, owner * width, width, 0)
+        wkv = lax.dynamic_slice_in_dim(keyvalue_weight, owner * width, width, 0)
+        return (
+            jnp.dot(normed, wq, preferred_element_type=jnp.float32),
+            jnp.dot(normed, wkv, preferred_element_type=jnp.float32),
+        )
+
+    held = {chain: state_halves[chain[1]] for chain in chains}
+    sums = [None, None]
+
+    def add_to(half, pair):
+        old = sums[half]
+        sums[half] = pair if old is None else (old[0] + pair[0], old[1] + pair[1])
+
+    output_cols = w_output.reshape(w_output.shape[0], size, w_output.shape[3])
+    out_blocks = jnp.transpose(output_cols, (1, 0, 2))
+    for step in range(1, long_way + 1):
+        arrived = {}
+        for chain in chains:
+            if step <= reach[chain]:
+                arrived[chain] = lax.ppermute(held[chain], "gx", hops[chain[0]])
+        if step == 1:
+            for half in (0, 1):
+                add_to(half, project(state_halves[half], half, me))
+        if step == 2:
+            (out_blocks, last) = lax.optimization_barrier((out_blocks, arrived[chains[0]]))
+            arrived[chains[0]] = last
+        for chain, raw in arrived.items():
+            add_to(chain[1], project(raw, chain[1], at_place(-chain[0] * step)))
+        held.update(arrived)
+
+    joined = [jnp.concatenate([q, kv], axis=1).astype(jnp.bfloat16) for q, kv in sums]
+    pair = [(0, 1), (1, 0)]
+    from_other = lax.ppermute(joined[0], "gy", pair)
+    mine = (joined[1].astype(jnp.float32) + from_other.astype(jnp.float32)).astype(jnp.bfloat16)
+
+    query_width = w_query.shape[1]
+    rows_here = half_rows // size
+    spread = lax.all_to_all(
+        mine.reshape(size, rows_here, mine.shape[1]), "gx", split_axis=0, concat_axis=0, tiled=True
+    )
+    spread = jnp.transpose(spread, (1, 0, 2))
+    queries = spread[:, :, :query_width].reshape(rows_here, -1)
+    keyvals = spread[:, :, query_width:].reshape(rows_here, -1)
     key_span_width = keyvals.shape[1] // 2
     attended = attend(
         queries,
@@ -104,20 +171,32 @@
         cached_value_rows,
         lengths,
     )
-    head_rows = lax.all_to_all(attended, "gx", split_axis=1, concat_axis=0, tiled=True)
-    gathered = lax.all_gather(head_rows, "gy", axis=0, tiled=True)
-    out_block = w_output.shape[3]
-    output_cols = w_output.reshape(w_output.shape[0], -1)
-    partial_value = jnp.dot(gathered, output_cols, preferred_element_type=jnp.float32)
-    summed = lax.psum_scatter(
-        partial_value.reshape(partial_value.shape[0], 1 * lax.axis_size("gx"), out_block)
-        .transpose(1, 0, 2)
-        .astype(jnp.bfloat16),
-        "gx",
-        scatter_dimension=0,
-        tiled=True,
-    ).astype(jnp.float32)
-    return (states.astype(jnp.float32) + summed[0]).astype(jnp.bfloat16)
+    own_rows = lax.all_to_all(attended, "gx", split_axis=1, concat_axis=0, tiled=True)
+    other_rows = lax.ppermute(own_rows, "gy", pair)
+    head_rows = [other_rows, own_rows]
+
+    def term(half, dest):
+        block = lax.dynamic_index_in_dim(out_blocks, dest, 0, keepdims=False)
+        return jnp.dot(head_rows[half], block, preferred_element_type=jnp.float32)
+
+    moving = {}
+    for step in range(long_way, 0, -1):
+        for chain in chains[2:] + chains[:2]:
+            if step <= reach[chain]:
+                value = term(chain[1], at_place(chain[0] * step))
+                if chain in moving:
+                    value = value + moving[chain].astype(jnp.float32)
+                moving[chain] = lax.ppermute(value.astype(jnp.bfloat16), "gx", hops[chain[0]])
+    halves = []
+    for half in (0, 1):
+        total = state_halves[half].astype(jnp.float32) + term(half, me)
+        for chain in chains:
+            if chain[1] == half and chain in moving:
+                total = total + moving[chain].astype(jnp.float32)
+        halves.append(total.astype(jnp.bfloat16))
+    out = jnp.zeros((row_count, width), jnp.bfloat16)
+    out = lax.dynamic_update_slice(out, halves[0], (other * half_rows, 0))
+    return lax.dynamic_update_slice(out, halves[1], (core * half_rows, 0))
 
 
 def solution(mesh):

time: 727 us -> 515 us (0.71); the launches traced: 725 us -> 506 us
  waiting for transfers between devices: 512 us -> 248 us
  matrix products: 63.1 us -> 114 us
  blocking collectives: 70.7 us -> 29.4 us
  starting transfers between devices: 4.12 us -> 38.3 us
  between operations: 13.3 us -> 38.9 us
  local copies, waits for them, and re-layouts: 47.3 us -> 29.9 us
    reduce_scatter x3 -> x0, waiting for transfers between devices: 282 us -> none  [the longest x1 282 us: shards(): lax.psum_scatter(partial_value.reshape(partial_value.shape[0], 1 * lax.ax...]
    all_gather x2 -> x0, waiting for transfers between devices: 205 us -> none  [the longest x1 205 us: shards(): lax.all_gather(states, 'gx', axis=1, tiled=True)]
    ppermute x0 -> x30, waiting for transfers between devices: none -> 165 us  [the longest x14 104 us: shards(): lax.ppermute(value.astype(jnp.bfloat16), 'gx', hops[chain[0]])]
    psum x0 -> x1, waiting for transfers between devices: none -> 53.5 us  [shards(): lax.psum(jnp.concatenate([jnp.sum(states_f * states_f, axis=1), gain_all]...]
    dot_general x3 -> x48, matrix products: 57.7 us -> 107 us  [the longest x16 43.7 us: project(): jnp.dot(normed, wq, preferred_element_type=jnp.float32)]
    ppermute x0 -> x30, starting transfers between devices: none -> 33.6 us  [the longest x14 18.3 us: shards(): arrived[chain] = lax.ppermute(held[chain], 'gx', hops[chain[0]])]
    all_gather x1 -> x0, blocking collectives: 28.1 us -> none  [shards(): lax.all_gather(norm_gain, 'gx', axis=0, tiled=True)]
    dot_general x1 -> x0, local copies, waits for them, and re-layouts: 22.4 us -> none  [shards(): jnp.dot(gathered, output_cols, preferred_element_type=jnp.float32)]
  transfers between devices with their start and end apart: 6 -> 32, of which waited for: 3 -> 16; matrix products, arithmetic and copies ran while one was open for 9% -> 25% of each run, Pallas kernels for 0% -> 0%
where the time goes in v1:
time: 515 us; the launch traced here: 506 us
  waiting for transfers between devices  248 us (48%)
  matrix products  114 us (22%)
  between operations  38.9 us (8%)
  starting transfers between devices  38.3 us (7%)
  local copies, waits for them, and re-layouts  29.9 us (6%)
  blocking collectives  29.4 us (6%)
  other arithmetic  8.2 us (2%)
    ppermute x14, waiting for transfers between devices, shards(): lax.ppermute(value.astype(jnp.bfloat16), 'gx', hops[chain[0]])  104 us
    ppermute x14, waiting for transfers between devices, shards(): arrived[chain] = lax.ppermute(held[chain], 'gx', hops[chain[0]])  60.6 us
    psum x1, waiting for transfers between devices, shards(): lax.psum(jnp.concatenate([jnp.sum(states_f * states_f, axis=1), gain_all]...  53.5 us
    dot_general x16, matrix products, project(): jnp.dot(normed, wq, preferred_element_type=jnp.float32)  43.7 us
    dot_general x16, matrix products, term(): return jnp.dot(head_rows[half], block, preferred_element_type=jnp.float32)  40.4 us
    all_to_all x1, blocking collectives, shards(): lax.all_to_all(attended, 'gx', split_axis=1, concat_axis=0, tiled=True)  29.4 us
    all_to_all x1, waiting for transfers between devices, shards(): lax.all_to_all(mine.reshape(size, rows_here, mine.shape[1]), 'gx', split_...  28.8 us
    dot_general x16, matrix products, project(): jnp.dot(normed, wkv, preferred_element_type=jnp.float32)  23 us
  transfers between devices with their start and end apart: 32, of which 16 were waited for; matrix products, arithmetic and copies ran while one was open for 25% of the time, Pallas kernels for 0%

profile of v1, /device:TPU:0, one launch (start us, length us, event | category | flops | bytes accessed | tf_op | source)
XLA Modules:
  0.0 506.1 jit_solution(15709633565810835715)
XLA Ops:
  12.3 3.0 collective-permute-start.7
  28.2 18.7 %copy.89 = bf16[1024,1,8,1024]{3,0,2,1:T(8,128)(2,1)} copy(bf16[1024,1,8,1024]{3,2,1,0:T(8,128)(2,1)} %param.14) | data formatting | bytes 33554432 | tf_op args[4]
  46.9 53.5 %all-reduce.2.cloned.1.call-done = f32[17408]{0:T(1024)} async-done(((f32[17408]{0:T(1024)}), f32[17408]{0:T(1024)}) %all-reduce.2.cloned.1.call-update) | async-done | bytes 69648 | tf_op jit(solution)/shard_map/psum | solution.py:109
  104.4 3.5 fusion.87
  110.7 3.3 collective-permute-start.9
  116.6 3.4 fusion.83
  119.9 3.2 fusion.79
  140.3 19.7 %collective-permute-done.3 = bf16[512,1024]{1,0:T(8,128)(2,1)S(1)} collective-permute-done((bf16[512,1024]{1,0:T(8,128)(2,1)}, bf16[512,1024]{1,0:T(8,128)(2,1)S(1)}, u32[]{:S(2)}, u32[]{:S(2)}) %collective-permute-start.3) | collective-permute-done | bytes 1048608 | tf_op jit(solution)/shard_map/ppermute | solution.py:141
  170.2 12.6 %collective-permute-done.11 = bf16[512,1024]{1,0:T(8,128)(2,1)} collective-permute-done((bf16[512,1024]{1,0:T(8,128)(2,1)S(1)}, bf16[512,1024]{1,0:T(8,128)(2,1)}, u32[]{:S(2)}, u32[]{:S(2)}) %collective-permute-start.11) | collective-permute-done | bytes 1048608 | tf_op jit(solution)/shard_map/ppermute | solution.py:141
  197.5 7.7 %collective-permute-done.4 = bf16[512,1024]{1,0:T(8,128)(2,1)} collective-permute-done((bf16[512,1024]{1,0:T(8,128)(2,1)S(1)}, bf16[512,1024]{1,0:T(8,128)(2,1)}, u32[]{:S(2)}, u32[]{:S(2)}) %collective-permute-start.4) | collective-permute-done | bytes 1048608 | tf_op jit(solution)/shard_map/ppermute | solution.py:141
  207.8 17.8 %collective-permute-done.13 = bf16[512,1024]{1,0:T(8,128)(2,1)} collective-permute-done((bf16[512,1024]{1,0:T(8,128)(2,1)}, bf16[512,1024]{1,0:T(8,128)(2,1)}, u32[]{:S(2)}, u32[]{:S(2)}) %collective-permute-start.13) | collective-permute-done | bytes 1048608 | tf_op jit(solution)/shard_map/ppermute | solution.py:141
  225.6 3.9 fusion.44
  229.4 4.4 add_convert_fusion.12
  239.8 3.3 add_convert_fusion.13
  244.5 4.7 all-to-all-start
  249.5 28.8 %all-to-all-done = bf16[8,64,1152]{2,1,0:T(8,128)(2,1)S(1)} async-done(((bf16[8,64,1152]{2,1,0:T(8,128)(2,1)}), bf16[8,64,1152]{2,1,0:T(8,128)(2,1)S(1)}, u32[]{:S(2)}, u32[]{:S(2)}) %all-to-all-start) | async-done | bytes 1179680 | tf_op jit(solution)/shard_map/all_to_all | solution.py:159
  289.4 3.4 divide_convert_fusion
  293.9 29.4 %all_to_all.24 = bf16[64,8,1024]{2,0,1:T(8,128)(2,1)S(1)} all-to-all(bf16[64,8,1024]{2,0,1:T(8,128)(2,1)S(1)} %copy.65), channel_id=1, replica_groups=mesh['groups'=2,'gx'=8,'gy'=2] {'gx'}, dimensions={1} | all-to-all | bytes 2097152 | tf_op jit(solution)/shard_map/all_to_all | solution.py:174
  325.9 3.9 fusion.94
  340.6 3.8 fusion.97
  345.9 9.4 %collective-permute-done.16 = bf16[512,1024]{1,0:T(8,128)(2,1)} collective-permute-done((bf16[512,1024]{1,0:T(8,128)(2,1)}, bf16[512,1024]{1,0:T(8,128)(2,1)}, u32[]{:S(2)}, u32[]{:S(2)}) %collective-permute-start.16) | collective-permute-done | bytes 1048608 | tf_op jit(solution)/shard_map/ppermute | solution.py:189
  355.3 4.1 add_convert_fusion.10
  367.6 3.0 fusion.91
  371.3 3.4 add_convert_fusion.3
  376.0 8.6 %collective-permute-done.20 = bf16[512,1024]{1,0:T(8,128)(2,1)} collective-permute-done((bf16[512,1024]{1,0:T(8,128)(2,1)}, bf16[512,1024]{1,0:T(8,128)(2,1)}, u32[]{:S(2)}, u32[]{:S(2)}) %collective-permute-start.20) | collective-permute-done | bytes 1048608 | tf_op jit(solution)/shard_map/ppermute | solution.py:189
  384.5 3.1 add_convert_fusion.7
  388.6 3.4 add_convert_fusion.9
  392.9 15.3 %collective-permute-done.23 = bf16[512,1024]{1,0:T(8,128)(2,1)S(1)} collective-permute-done((bf16[512,1024]{1,0:T(8,128)(2,1)S(1)}, bf16[512,1024]{1,0:T(8,128)(2,1)S(1)}, u32[]{:S(2)}, u32[]{:S(2)}) %collective-permute-start.23) | collective-permute-done | bytes 1048608 | tf_op jit(solution)/shard_map/ppermute | solution.py:189
  412.9 16.4 %collective-permute-done.21 = bf16[512,1024]{1,0:T(8,128)(2,1)S(1)} collective-permute-done((bf16[512,1024]{1,0:T(8,128)(2,1)S(1)}, bf16[512,1024]{1,0:T(8,128)(2,1)S(1)}, u32[]{:S(2)}, u32[]{:S(2)}) %collective-permute-start.21) | collective-permute-done | bytes 1048608 | tf_op jit(solution)/shard_map/ppermute | solution.py:189
  434.1 19.1 %collective-permute-done.24 = bf16[512,1024]{1,0:T(8,128)(2,1)S(1)} collective-permute-done((bf16[512,1024]{1,0:T(8,128)(2,1)S(1)}, bf16[512,1024]{1,0:T(8,128)(2,1)S(1)}, u32[]{:S(2)}, u32[]{:S(2)}) %collective-permute-start.24) | collective-permute-done | bytes 1048608 | tf_op jit(solution)/shard_map/ppermute | solution.py:189
  458.1 16.2 %collective-permute-done.22 = bf16[512,1024]{1,0:T(8,128)(2,1)S(1)} collective-permute-done((bf16[512,1024]{1,0:T(8,128)(2,1)S(1)}, bf16[512,1024]{1,0:T(8,128)(2,1)S(1)}, u32[]{:S(2)}, u32[]{:S(2)}) %collective-permute-start.22) | collective-permute-done | bytes 1048608 | tf_op jit(solution)/shard_map/ppermute | solution.py:189
  478.7 17.7 %collective-permute-done.25 = bf16[512,1024]{1,0:T(8,128)(2,1)S(1)} collective-permute-done((bf16[512,1024]{1,0:T(8,128)(2,1)S(1)}, bf16[512,1024]{1,0:T(8,128)(2,1)S(1)}, u32[]{:S(2)}, u32[]{:S(2)}) %collective-permute-start.25) | collective-permute-done | bytes 1048608 | tf_op jit(solution)/shard_map/ppermute | solution.py:189
  (162 shorter events, 115.7 us)
Async XLA Ops:
  6.5 93.9 %all-reduce.2.cloned.1.call-start = ((), (), s32[]{:S(2)}) async-start(), calls=%async_computation.2 | async-start | bytes 139264 | tf_op jit(solution)/shard_map/psum | solution.py:109
  12.3 98.5 %collective-permute-start.7 = (bf16[512,1024]{1,0:T(8,128)(2,1)}, bf16[512,1024]{1,0:T(8,128)(2,1)}, u32[]{:S(2)}, u32[]{:S(2)}) collective-permute-start(bf16[512,1024]{1,0:T(8,128)(2,1)} %get-tuple-element.12), channel_id=1, source_target_pairs={{0,4},{4,8},{8,12},{12,14},{14,10},{10,6},{6,2},{2,0},{1,5},{5,9},... | collective-permute-start | bytes 3145736 | tf_op jit(solution)/shard_map/ppermute | solution.py:141
  15.3 98.7 %collective-permute-start.8 = (bf16[512,1024]{1,0:T(8,128)(2,1)}, bf16[512,1024]{1,0:T(8,128)(2,1)}, u32[]{:S(2)}, u32[]{:S(2)}) collective-permute-start(bf16[512,1024]{1,0:T(8,128)(2,1)} %get-tuple-element.12), channel_id=1, source_target_pairs={{4,0},{8,4},{12,8},{14,12},{10,14},{6,10},{2,6},{0,2},{5,1},{9,5},... | collective-permute-start | bytes 3145736 | tf_op jit(solution)/shard_map/ppermute | solution.py:141
  15.3 98.8 %collective-permute-start.1 = (bf16[512,1024]{1,0:T(8,128)(2,1)S(1)}, bf16[512,1024]{1,0:T(8,128)(2,1)}, u32[]{:S(2)}, u32[]{:S(2)}) collective-permute-start(bf16[512,1024]{1,0:T(8,128)(2,1)S(1)} %get-tuple-element.11), channel_id=1, source_target_pairs={{4,0},{8,4},{12,8},{14,12},{10,14},{6,10},{2,6},{0,2},{5,1},{9,5},... | collective-permute-start | bytes 3145736 | tf_op jit(solution)/shard_map/ppermute | solution.py:141
  17.3 108.5 %collective-permute-start = (bf16[512,1024]{1,0:T(8,128)(2,1)S(1)}, bf16[512,1024]{1,0:T(8,128)(2,1)}, u32[]{:S(2)}, u32[]{:S(2)}) collective-permute-start(bf16[512,1024]{1,0:T(8,128)(2,1)S(1)} %get-tuple-element.11), channel_id=1, source_target_pairs={{0,4},{4,8},{8,12},{12,14},{14,10},{10,6},{6,2},{2,0},{1,5},{5,9},... | collective-permute-start | bytes 3145736 | tf_op jit(solution)/shard_map/ppermute | solution.py:141
  110.7 27.2 %collective-permute-start.9 = (bf16[512,1024]{1,0:T(8,128)(2,1)}, bf16[512,1024]{1,0:T(8,128)(2,1)S(1)}, u32[]{:S(2)}, u32[]{:S(2)}) collective-permute-start(bf16[512,1024]{1,0:T(8,128)(2,1)} %collective-permute-done.7), channel_id=1, source_target_pairs={{0,4},{4,8},{8,12},{12,14},{14,10},{10,6},{6,2},{2,0},{1,5},{5,9},... | collective-permute-start | bytes 3145736 | tf_op jit(solution)/shard_map/ppermute | solution.py:141
  114.0 47.8 %collective-permute-start.10 = (bf16[512,1024]{1,0:T(8,128)(2,1)}, bf16[512,1024]{1,0:T(8,128)(2,1)}, u32[]{:S(2)}, u32[]{:S(2)}) collective-permute-start(bf16[512,1024]{1,0:T(8,128)(2,1)} %collective-permute-done.8), channel_id=1, source_target_pairs={{4,0},{8,4},{12,8},{14,12},{10,14},{6,10},{2,6},{0,2},{5,1},{9,5},... | collective-permute-start | bytes 3145736 | tf_op jit(solution)/shard_map/ppermute | solution.py:141
  114.0 46.0 %collective-permute-start.3 = (bf16[512,1024]{1,0:T(8,128)(2,1)}, bf16[512,1024]{1,0:T(8,128)(2,1)S(1)}, u32[]{:S(2)}, u32[]{:S(2)}) collective-permute-start(bf16[512,1024]{1,0:T(8,128)(2,1)} %collective-permute-done.1), channel_id=1, source_target_pairs={{4,0},{8,4},{12,8},{14,12},{10,14},{6,10},{2,6},{0,2},{5,1},{9,5},... | collective-permute-start | bytes 3145736 | tf_op jit(solution)/shard_map/ppermute | solution.py:141
  125.8 38.6 %collective-permute-start.2 = (bf16[512,1024]{1,0:T(8,128)(2,1)}, bf16[512,1024]{1,0:T(8,128)(2,1)S(1)}, u32[]{:S(2)}, u32[]{:S(2)}) collective-permute-start(bf16[512,1024]{1,0:T(8,128)(2,1)} %collective-permute-done), channel_id=1, source_target_pairs={{0,4},{4,8},{8,12},{12,14},{14,10},{10,6},{6,2},{2,0},{1,5},{5,9},... | collective-permute-start | bytes 3145736 | tf_op jit(solution)/shard_map/ppermute | solution.py:141
  138.0 44.8 %collective-permute-start.11 = (bf16[512,1024]{1,0:T(8,128)(2,1)S(1)}, bf16[512,1024]{1,0:T(8,128)(2,1)}, u32[]{:S(2)}, u32[]{:S(2)}) collective-permute-start(bf16[512,1024]{1,0:T(8,128)(2,1)S(1)} %collective-permute-done.9), channel_id=1, source_target_pairs={{0,4},{4,8},{8,12},{12,14},{14,10},{10,6},{6,2},{2,0},{1,5},{5,9},... | collective-permute-start | bytes 3145736 | tf_op jit(solution)/shard_map/ppermute | solution.py:141
  160.0 27.9 %collective-permute-start.5 = (bf16[512,1024]{1,0:T(8,128)(2,1)S(1)}, bf16[512,1024]{1,0:T(8,128)(2,1)}, u32[]{:S(2)}, u32[]{:S(2)}) collective-permute-start(bf16[512,1024]{1,0:T(8,128)(2,1)S(1)} %collective-permute-done.3), channel_id=1, source_target_pairs={{4,0},{8,4},{12,8},{14,12},{10,14},{6,10},{2,6},{0,2},{5,1},{9,5},... | collective-permute-start | bytes 3145736 | tf_op jit(solution)/shard_map/ppermute | solution.py:141
  164.4 40.8 %collective-permute-start.4 = (bf16[512,1024]{1,0:T(8,128)(2,1)S(1)}, bf16[512,1024]{1,0:T(8,128)(2,1)}, u32[]{:S(2)}, u32[]{:S(2)}) collective-permute-start(bf16[512,1024]{1,0:T(8,128)(2,1)S(1)} %collective-permute-done.2), channel_id=1, source_target_pairs={{0,4},{4,8},{8,12},{12,14},{14,10},{10,6},{6,2},{2,0},{1,5},{5,9},... | collective-permute-start | bytes 3145736 | tf_op jit(solution)/shard_map/ppermute | solution.py:141
  167.5 61.9 %collective-permute-start.12 = (bf16[512,1024]{1,0:T(8,128)(2,1)}, bf16[512,1024]{1,0:T(8,128)(2,1)}, u32[]{:S(2)}, u32[]{:S(2)}) collective-permute-start(bf16[512,1024]{1,0:T(8,128)(2,1)} %collective-permute-done.10), channel_id=1, source_target_pairs={{4,0},{8,4},{12,8},{14,12},{10,14},{6,10},{2,6},{0,2},{5,1},{9,5},... | collective-permute-start | bytes 3145736 | tf_op jit(solution)/shard_map/ppermute | solution.py:141
  182.8 42.8 %collective-permute-start.13 = (bf16[512,1024]{1,0:T(8,128)(2,1)}, bf16[512,1024]{1,0:T(8,128)(2,1)}, u32[]{:S(2)}, u32[]{:S(2)}) collective-permute-start(bf16[512,1024]{1,0:T(8,128)(2,1)} %collective-permute-done.11), channel_id=1, source_target_pairs={{0,4},{4,8},{8,12},{12,14},{14,10},{10,6},{6,2},{2,0},{1,5},{5,9},... | collective-permute-start | bytes 3145736 | tf_op jit(solution)/shard_map/ppermute | solution.py:141
  188.0 51.3 %collective-permute-start.6 = (bf16[512,1024]{1,0:T(8,128)(2,1)}, bf16[512,1024]{1,0:T(8,128)(2,1)S(1)}, u32[]{:S(2)}, u32[]{:S(2)}) collective-permute-start(bf16[512,1024]{1,0:T(8,128)(2,1)} %collective-permute-done.5), channel_id=1, source_target_pairs={{4,0},{8,4},{12,8},{14,12},{10,14},{6,10},{2,6},{0,2},{5,1},{9,5},... | collective-permute-start | bytes 3145736 | tf_op jit(solution)/shard_map/ppermute | solution.py:141
  237.5 5.7 %collective-permute-start.14 = (bf16[512,1152]{1,0:T(8,128)(2,1)S(1)}, bf16[512,1152]{1,0:T(8,128)(2,1)S(1)}, u32[]{:S(2)}, u32[]{:S(2)}) collective-permute-start(bf16[512,1152]{1,0:T(8,128)(2,1)S(1)} %pad_maximum_fusion), channel_id=1, source_target_pairs={{0,1},{1,0},{2,3},{3,2},{4,5},{5,4},{6,7},{7,6},{8,9},{9,8},{10,11... | collective-permute-start | bytes 3538952 | tf_op jit(solution)/shard_map/ppermute | solution.py:154
  244.5 33.8 %all-to-all-start = ((bf16[8,64,1152]{2,1,0:T(8,128)(2,1)}), bf16[8,64,1152]{2,1,0:T(8,128)(2,1)S(1)}, u32[]{:S(2)}, u32[]{:S(2)}) async-start(bf16[8,64,1152]{2,1,0:T(8,128)(2,1)} %bitcast.18), calls=%async_computation | async-start | bytes 2359296 | tf_op jit(solution)/shard_map/all_to_all | solution.py:159
  323.3 2.7 collective-permute-start.15
  329.8 25.5 %collective-permute-start.16 = (bf16[512,1024]{1,0:T(8,128)(2,1)}, bf16[512,1024]{1,0:T(8,128)(2,1)}, u32[]{:S(2)}, u32[]{:S(2)}) collective-permute-start(bf16[512,1024]{1,0:T(8,128)(2,1)} %fusion.94), channel_id=1, source_target_pairs={{0,4},{4,8},{8,12},{12,14},{14,10},{10,6},{6,2},{2,0},{1,5},{5,9},... | collective-permute-start | bytes 3145736 | tf_op jit(solution)/shard_map/ppermute | solution.py:189
  335.7 35.6 %collective-permute-start.26 = (bf16[512,1024]{1,0:T(8,128)(2,1)S(1)}, bf16[512,1024]{1,0:T(8,128)(2,1)}, u32[]{:S(2)}, u32[]{:S(2)}) collective-permute-start(bf16[512,1024]{1,0:T(8,128)(2,1)S(1)} %fusion.100), channel_id=1, source_target_pairs={{4,0},{8,4},{12,8},{14,12},{10,14},{6,10},{2,6},{0,2},{5,1},{9,5},... | collective-permute-start | bytes 3145736 | tf_op jit(solution)/shard_map/ppermute | solution.py:189
  344.4 40.1 %collective-permute-start.20 = (bf16[512,1024]{1,0:T(8,128)(2,1)}, bf16[512,1024]{1,0:T(8,128)(2,1)}, u32[]{:S(2)}, u32[]{:S(2)}) collective-permute-start(bf16[512,1024]{1,0:T(8,128)(2,1)} %fusion.97), channel_id=1, source_target_pairs={{4,0},{8,4},{12,8},{14,12},{10,14},{6,10},{2,6},{0,2},{5,1},{9,5},... | collective-permute-start | bytes 3145736 | tf_op jit(solution)/shard_map/ppermute | solution.py:189
  359.4 29.2 %collective-permute-start.17 = (bf16[512,1024]{1,0:T(8,128)(2,1)}, bf16[512,1024]{1,0:T(8,128)(2,1)}, u32[]{:S(2)}, u32[]{:S(2)}) collective-permute-start(bf16[512,1024]{1,0:T(8,128)(2,1)} %add_convert_fusion.10), channel_id=1, source_target_pairs={{0,4},{4,8},{8,12},{12,14},{14,10},{10,6},{6,2},{2,0},{1,5},{5,9},... | collective-permute-start | bytes 3145736 | tf_op jit(solution)/shard_map/ppermute | solution.py:189
  370.6 37.6 %collective-permute-start.23 = (bf16[512,1024]{1,0:T(8,128)(2,1)S(1)}, bf16[512,1024]{1,0:T(8,128)(2,1)S(1)}, u32[]{:S(2)}, u32[]{:S(2)}) collective-permute-start(bf16[512,1024]{1,0:T(8,128)(2,1)S(1)} %fusion.91), channel_id=1, source_target_pairs={{0,4},{4,8},{8,12},{12,14},{14,10},{10,6},{6,2},{2,0},{1,5},{5,9},... | collective-permute-start | bytes 3145736 | tf_op jit(solution)/shard_map/ppermute | solution.py:189
  374.7 36.0 %collective-permute-start.27 = (bf16[512,1024]{1,0:T(8,128)(2,1)S(1)}, bf16[512,1024]{1,0:T(8,128)(2,1)S(1)}, u32[]{:S(2)}, u32[]{:S(2)}) collective-permute-start(bf16[512,1024]{1,0:T(8,128)(2,1)S(1)} %add_convert_fusion.3), channel_id=1, source_target_pairs={{4,0},{8,4},{12,8},{14,12},{10,14},{6,10},{2,6},{0,2},{5,1},{9,5},... | collective-permute-start | bytes 3145736 | tf_op jit(solution)/shard_map/ppermute | solution.py:189
  387.7 41.7 %collective-permute-start.21 = (bf16[512,1024]{1,0:T(8,128)(2,1)S(1)}, bf16[512,1024]{1,0:T(8,128)(2,1)S(1)}, u32[]{:S(2)}, u32[]{:S(2)}) collective-permute-start(bf16[512,1024]{1,0:T(8,128)(2,1)S(1)} %add_convert_fusion.7), channel_id=1, source_target_pairs={{4,0},{8,4},{12,8},{14,12},{10,14},{6,10},{2,6},{0,2},{5,1},{9,5},... | collective-permute-start | bytes 3145736 | tf_op jit(solution)/shard_map/ppermute | solution.py:189
  392.0 39.6 %collective-permute-start.18 = (bf16[512,1024]{1,0:T(8,128)(2,1)S(1)}, bf16[512,1024]{1,0:T(8,128)(2,1)S(1)}, u32[]{:S(2)}, u32[]{:S(2)}) collective-permute-start(bf16[512,1024]{1,0:T(8,128)(2,1)S(1)} %add_convert_fusion.9), channel_id=1, source_target_pairs={{0,4},{4,8},{8,12},{12,14},{14,10},{10,6},{6,2},{2,0},{1,5},{5,9},... | collective-permute-start | bytes 3145736 | tf_op jit(solution)/shard_map/ppermute | solution.py:189
  409.5 43.6 %collective-permute-start.24 = (bf16[512,1024]{1,0:T(8,128)(2,1)S(1)}, bf16[512,1024]{1,0:T(8,128)(2,1)S(1)}, u32[]{:S(2)}, u32[]{:S(2)}) collective-permute-start(bf16[512,1024]{1,0:T(8,128)(2,1)S(1)} %add_convert_fusion.5), channel_id=1, source_target_pairs={{0,4},{4,8},{8,12},{12,14},{14,10},{10,6},{6,2},{2,0},{1,5},{5,9},... | collective-permute-start | bytes 3145736 | tf_op jit(solution)/shard_map/ppermute | solution.py:189
  412.0 43.9 %collective-permute-start.28 = (bf16[512,1024]{1,0:T(8,128)(2,1)S(1)}, bf16[512,1024]{1,0:T(8,128)(2,1)S(1)}, u32[]{:S(2)}, u32[]{:S(2)}) collective-permute-start(bf16[512,1024]{1,0:T(8,128)(2,1)S(1)} %add_convert_fusion.2), channel_id=1, source_target_pairs={{4,0},{8,4},{12,8},{14,12},{10,14},{6,10},{2,6},{0,2},{5,1},{9,5},... | collective-permute-start | bytes 3145736 | tf_op jit(solution)/shard_map/ppermute | solution.py:189
  430.7 43.7 %collective-permute-start.22 = (bf16[512,1024]{1,0:T(8,128)(2,1)S(1)}, bf16[512,1024]{1,0:T(8,128)(2,1)S(1)}, u32[]{:S(2)}, u32[]{:S(2)}) collective-permute-start(bf16[512,1024]{1,0:T(8,128)(2,1)S(1)} %add_convert_fusion.6), channel_id=1, source_target_pairs={{4,0},{8,4},{12,8},{14,12},{10,14},{6,10},{2,6},{0,2},{5,1},{9,5},... | collective-permute-start | bytes 3145736 | tf_op jit(solution)/shard_map/ppermute | solution.py:189
  432.9 42.7 %collective-permute-start.19 = (bf16[512,1024]{1,0:T(8,128)(2,1)S(1)}, bf16[512,1024]{1,0:T(8,128)(2,1)S(1)}, u32[]{:S(2)}, u32[]{:S(2)}) collective-permute-start(bf16[512,1024]{1,0:T(8,128)(2,1)S(1)} %add_convert_fusion.8), channel_id=1, source_target_pairs={{0,4},{4,8},{8,12},{12,14},{14,10},{10,6},{6,2},{2,0},{1,5},{5,9},... | collective-permute-start | bytes 3145736 | tf_op jit(solution)/shard_map/ppermute | solution.py:189
  454.4 41.9 %collective-permute-start.25 = (bf16[512,1024]{1,0:T(8,128)(2,1)S(1)}, bf16[512,1024]{1,0:T(8,128)(2,1)S(1)}, u32[]{:S(2)}, u32[]{:S(2)}) collective-permute-start(bf16[512,1024]{1,0:T(8,128)(2,1)S(1)} %add_convert_fusion.4), channel_id=1, source_target_pairs={{0,4},{4,8},{8,12},{12,14},{14,10},{10,6},{6,2},{2,0},{1,5},{5,9},... | collective-permute-start | bytes 3145736 | tf_op jit(solution)/shard_map/ppermute | solution.py:189
  457.1 39.2 %collective-permute-start.29 = (bf16[512,1024]{1,0:T(8,128)(2,1)S(1)}, bf16[512,1024]{1,0:T(8,128)(2,1)S(1)}, u32[]{:S(2)}, u32[]{:S(2)}) collective-permute-start(bf16[512,1024]{1,0:T(8,128)(2,1)S(1)} %add_convert_fusion.1), channel_id=1, source_target_pairs={{4,0},{8,4},{12,8},{14,12},{10,14},{6,10},{2,6},{0,2},{5,1},{9,5},... | collective-permute-start | bytes 3145736 | tf_op jit(solution)/shard_map/ppermute | solution.py:189
  (20 other events, 452.4 us)
Sparse Core Ops, SparseCore 0:
  10.8 89.5 all-reduce.1

commit v2 on v1

--- a/solution.py
+++ b/solution.py
@@ -102,15 +102,21 @@
     state_halves = [half_of(states, 0), half_of(states, 1)]
 
     states_f = states.astype(jnp.float32)
-    gain_all = jnp.zeros((2 * size * width,), jnp.float32)
     gain_all = lax.dynamic_update_slice(
-        gain_all, norm_gain.astype(jnp.float32), ((core * size + me) * width,)
-    )
-    both = lax.psum(
-        jnp.concatenate([jnp.sum(states_f * states_f, axis=1), gain_all]), ("gx", "gy")
-    )
-    norm_scale = lax.rsqrt(both[:row_count] / MODEL_WIDTH + epsilon)
-    gain_mine = lax.dynamic_slice_in_dim(both[row_count:], core * size * width, size * width, 0)
+        jnp.zeros((size * width,), jnp.float32), norm_gain.astype(jnp.float32), (me * width,)
+    )
+    both = jnp.concatenate([jnp.sum(states_f * states_f, axis=1), gain_all])
+    if size & (size - 1) == 0:
+        stride = 1
+        while stride < size:
+            both = both + lax.ppermute(both, "gx", [(i, i ^ stride) for i in range(size)])
+            stride *= 2
+    else:
+        both = lax.psum(both, "gx")
+    squares = both[:row_count]
+    squares = squares + lax.ppermute(squares, "gy", [(0, 1), (1, 0)])
+    norm_scale = lax.rsqrt(squares / MODEL_WIDTH + epsilon)
+    gain_mine = both[row_count:]
     scale_halves = [half_of(norm_scale, 0), half_of(norm_scale, 1)]
 
     def project(raw, half, owner):
@@ -132,8 +138,17 @@
         old = sums[half]
         sums[half] = pair if old is None else (old[0] + pair[0], old[1] + pair[1])
 
-    output_cols = w_output.reshape(w_output.shape[0], size, w_output.shape[3])
-    out_blocks = jnp.transpose(output_cols, (1, 0, 2))
+    out_blocks = {}
+
+    def load_block(offset, after):
+        weight, after = lax.optimization_barrier((w_output, after))
+        block = lax.dynamic_index_in_dim(weight[:, 0], at_place(offset), 1, keepdims=False)
+        block, after = lax.optimization_barrier((block, after))
+        out_blocks[offset % size] = block
+        return after
+
+    offsets = list(range(size))
+    per_step = -(-size // long_way)
     for step in range(1, long_way + 1):
         arrived = {}
         for chain in chains:
@@ -142,9 +157,9 @@
         if step == 1:
             for half in (0, 1):
                 add_to(half, project(state_halves[half], half, me))
-        if step == 2:
-            (out_blocks, last) = lax.optimization_barrier((out_blocks, arrived[chains[0]]))
-            arrived[chains[0]] = last
+        for offset in offsets[(step - 1) * per_step : step * per_step]:
+            held_first = chains[0] if chains[0] in arrived else chains[1]
+            arrived[held_first] = load_block(offset, arrived[held_first])
         for chain, raw in arrived.items():
             add_to(chain[1], project(raw, chain[1], at_place(-chain[0] * step)))
         held.update(arrived)
@@ -176,20 +191,21 @@
     head_rows = [other_rows, own_rows]
 
     def term(half, dest):
-        block = lax.dynamic_index_in_dim(out_blocks, dest, 0, keepdims=False)
-        return jnp.dot(head_rows[half], block, preferred_element_type=jnp.float32)
+        return jnp.dot(
+            head_rows[half], out_blocks[dest % size], preferred_element_type=jnp.float32
+        )
 
     moving = {}
     for step in range(long_way, 0, -1):
         for chain in chains[2:] + chains[:2]:
             if step <= reach[chain]:
-                value = term(chain[1], at_place(chain[0] * step))
+                value = term(chain[1], chain[0] * step)
                 if chain in moving:
                     value = value + moving[chain].astype(jnp.float32)
                 moving[chain] = lax.ppermute(value.astype(jnp.bfloat16), "gx", hops[chain[0]])
     halves = []
     for half in (0, 1):
-        total = state_halves[half].astype(jnp.float32) + term(half, me)
+        total = state_halves[half].astype(jnp.float32) + term(half, 0)
         for chain in chains:
             if chain[1] == half and chain in moving:
                 total = total + moving[chain].astype(jnp.float32)

time: 515 us -> 640 us (1.24)
  local copies, waits for them, and re-layouts: 29.9 us -> 227 us
  waiting for transfers between devices: 248 us -> 167 us
  matrix products: 114 us -> 125 us
  between operations: 38.9 us -> 29.2 us
    optimization_barrier x0 -> x8, local copies, waits for them, and re-layouts: none -> 201 us  [load_block(): weight, after = lax.optimization_barrier((w_output, after))]
    ppermute x14, waiting for transfers between devices: 60.6 us -> 1.6 us  [shards(): arrived[chain] = lax.ppermute(held[chain], 'gx', hops[chain[0]])]
    psum x1 -> x0, waiting for transfers between devices: 53.5 us -> none  [shards(): lax.psum(jnp.concatenate([jnp.sum(states_f * states_f, axis=1), gain_all]...]
    ppermute x14, waiting for transfers between devices: 104 us -> 132 us  [shards(): lax.ppermute(value.astype(jnp.bfloat16), 'gx', hops[chain[0]])]
    dot_general x16, matrix products: 43.7 us -> 66.4 us  [project(): jnp.dot(normed, wq, preferred_element_type=jnp.float32)]
    dot_general x16, matrix products: 40.4 us -> 21.7 us  [term(): jnp.dot(head_rows[half], out_blocks[dest % size], preferred_element_type=...]
    unnamed x41 -> x58, local copies, waits for them, and re-layouts: 19.1 us -> 2.12 us
    squeeze x0 -> x8, local copies, waits for them, and re-layouts: none -> 12.2 us  [load_block(): lax.dynamic_index_in_dim(weight[:, 0], at_place(offset), 1, keepdims=False)]
  transfers between devices with their start and end apart: 32 -> 35, of which waited for: 16 -> 15; matrix products, arithmetic and copies ran while one was open for 25% -> 53% of each run, Pallas kernels for 0% -> 0%
where the time goes in v2:
time: 640 us; the launch traced here: 632 us
  local copies, waits for them, and re-layouts  227 us (35%)
  waiting for transfers between devices  167 us (26%)
  matrix products  125 us (20%)
  starting transfers between devices  41.9 us (7%)
  blocking collectives  29.5 us (5%)
  between operations  29.2 us (5%)
  other arithmetic  12.1 us (2%)
    optimization_barrier x8, local copies, waits for them, and re-layouts, load_block(): weight, after = lax.optimization_barrier((w_output, after))  201 us
    ppermute x14, waiting for transfers between devices, shards(): lax.ppermute(value.astype(jnp.bfloat16), 'gx', hops[chain[0]])  132 us
    dot_general x16, matrix products, project(): jnp.dot(normed, wq, preferred_element_type=jnp.float32)  66.4 us
    all_to_all x1, blocking collectives, shards(): lax.all_to_all(attended, 'gx', split_axis=1, concat_axis=0, tiled=True)  29.5 us
    dot_general x16, matrix products, project(): jnp.dot(normed, wkv, preferred_element_type=jnp.float32)  29 us
    all_to_all x1, waiting for transfers between devices, shards(): lax.all_to_all(mine.reshape(size, rows_here, mine.shape[1]), 'gx', split_...  28.7 us
    dot_general x16, matrix products, term(): jnp.dot(head_rows[half], out_blocks[dest % size], preferred_element_type=...  21.7 us
    ppermute x14, starting transfers between devices, shards(): arrived[chain] = lax.ppermute(held[chain], 'gx', hops[chain[0]])  14.8 us
  transfers between devices with their start and end apart: 35, of which 15 were waited for; matrix products, arithmetic and copies ran while one was open for 53% of the time, Pallas kernels for 0%

profile of v2, /device:TPU:0, one launch (start us, length us, event | category | flops | bytes accessed | tf_op | source)
XLA Modules:
  0.0 631.9 jit_solution(13910741431964858719)
XLA Ops:
  54.1 3.8 fusion.39
  60.8 25.2 %copy.61 = bf16[1024,1,8,1024]{3,0,2,1:T(8,128)(2,1)S(1)} copy(bf16[1024,1,8,1024]{3,2,1,0:T(8,128)(2,1)S(1)} %copy-done.1) | data formatting | bytes 33554432 | tf_op jit(solution)/shard_map/optimization_barrier | solution.py:144
  87.5 25.1 %copy.62 = bf16[1024,1,8,1024]{3,0,2,1:T(8,128)(2,1)S(1)} copy(bf16[1024,1,8,1024]{3,2,1,0:T(8,128)(2,1)S(1)} %copy-done.1) | data formatting | bytes 33554432 | tf_op jit(solution)/shard_map/optimization_barrier | solution.py:144
  119.4 4.5 fusion.35
  123.9 4.6 fusion.31
  136.7 3.2 fusion.37
  140.4 25.1 %copy.63 = bf16[1024,1,8,1024]{3,0,2,1:T(8,128)(2,1)S(1)} copy(bf16[1024,1,8,1024]{3,2,1,0:T(8,128)(2,1)S(1)} %copy-done.1) | data formatting | bytes 33554432 | tf_op jit(solution)/shard_map/optimization_barrier | solution.py:144
  167.0 25.1 %copy.64 = bf16[1024,1,8,1024]{3,0,2,1:T(8,128)(2,1)S(1)} copy(bf16[1024,1,8,1024]{3,2,1,0:T(8,128)(2,1)S(1)} %copy-done.1) | data formatting | bytes 33554432 | tf_op jit(solution)/shard_map/optimization_barrier | solution.py:144
  199.0 4.6 fusion.27
  203.6 4.6 fusion.23
  212.8 4.6 fusion.25
  219.1 4.6 fusion.29
  223.7 25.1 %copy.65 = bf16[1024,1,8,1024]{3,0,2,1:T(8,128)(2,1)S(1)} copy(bf16[1024,1,8,1024]{3,2,1,0:T(8,128)(2,1)S(1)} %copy-done.1) | data formatting | bytes 33554432 | tf_op jit(solution)/shard_map/optimization_barrier | solution.py:144
  250.3 25.1 %copy.66 = bf16[1024,1,8,1024]{3,0,2,1:T(8,128)(2,1)S(1)} copy(bf16[1024,1,8,1024]{3,2,1,0:T(8,128)(2,1)S(1)} %copy-done.1) | data formatting | bytes 33554432 | tf_op jit(solution)/shard_map/optimization_barrier | solution.py:144
  278.4 4.5 fusion.19
  287.9 4.5 fusion.17
  294.2 4.5 fusion.21
  299.8 25.1 %copy.67 = bf16[1024,1,8,1024]{3,0,2,1:T(8,128)(2,1)S(1)} copy(bf16[1024,1,8,1024]{3,2,1,0:T(8,128)(2,1)S(1)} %copy-done.1) | data formatting | bytes 33554432 | tf_op jit(solution)/shard_map/optimization_barrier | solution.py:144
  326.3 25.1 %copy.68 = bf16[1024,1,8,1024]{3,0,2,1:T(8,128)(2,1)S(1)} copy(bf16[1024,1,8,1024]{3,2,1,0:T(8,128)(2,1)S(1)} %copy-done.1) | data formatting | bytes 33554432 | tf_op jit(solution)/shard_map/optimization_barrier | solution.py:144
  353.0 3.3 fusion.10
  356.8 5.1 add_convert_fusion.12
  369.5 3.6 add_convert_fusion.13
  374.5 4.0 all-to-all-start
  378.8 28.7 %all-to-all-done = bf16[8,64,1152]{2,1,0:T(8,128)(2,1)S(1)} async-done(((bf16[8,64,1152]{2,1,0:T(8,128)(2,1)}), bf16[8,64,1152]{2,1,0:T(8,128)(2,1)S(1)}, u32[]{:S(2)}, u32[]{:S(2)}) %all-to-all-start) | async-done | bytes 1179680 | tf_op jit(solution)/shard_map/all_to_all | solution.py:174
  423.0 4.6 divide_convert_fusion
  429.7 29.5 %all_to_all.24 = bf16[64,8,1024]{2,0,1:T(8,128)(2,1)S(1)} all-to-all(bf16[64,8,1024]{2,0,1:T(8,128)(2,1)S(1)} %copy.79), channel_id=1, replica_groups=mesh['groups'=2,'gx'=8,'gy'=2] {'gx'}, dimensions={1} | all-to-all | bytes 2097152 | tf_op jit(solution)/shard_map/all_to_all | solution.py:189
  471.7 39.4 %collective-permute-done.20 = bf16[512,1024]{1,0:T(8,128)(2,1)S(1)} collective-permute-done((bf16[512,1024]{1,0:T(8,128)(2,1)S(1)}, bf16[512,1024]{1,0:T(8,128)(2,1)S(1)}, u32[]{:S(2)}, u32[]{:S(2)}) %collective-permute-start.20) | collective-permute-done | bytes 1048608 | tf_op jit(solution)/shard_map/ppermute | solution.py:205
  518.7 18.2 %collective-permute-done.21 = bf16[512,1024]{1,0:T(8,128)(2,1)S(1)} collective-permute-done((bf16[512,1024]{1,0:T(8,128)(2,1)S(1)}, bf16[512,1024]{1,0:T(8,128)(2,1)S(1)}, u32[]{:S(2)}, u32[]{:S(2)}) %collective-permute-start.21) | collective-permute-done | bytes 1048608 | tf_op jit(solution)/shard_map/ppermute | solution.py:205
  543.6 20.6 %collective-permute-done.25 = bf16[512,1024]{1,0:T(8,128)(2,1)S(1)} collective-permute-done((bf16[512,1024]{1,0:T(8,128)(2,1)S(1)}, bf16[512,1024]{1,0:T(8,128)(2,1)S(1)}, u32[]{:S(2)}, u32[]{:S(2)}) %collective-permute-start.25) | collective-permute-done | bytes 1048608 | tf_op jit(solution)/shard_map/ppermute | solution.py:205
  569.1 17.7 %collective-permute-done.28 = bf16[512,1024]{1,0:T(8,128)(2,1)S(1)} collective-permute-done((bf16[512,1024]{1,0:T(8,128)(2,1)S(1)}, bf16[512,1024]{1,0:T(8,128)(2,1)S(1)}, u32[]{:S(2)}, u32[]{:S(2)}) %collective-permute-start.28) | collective-permute-done | bytes 1048608 | tf_op jit(solution)/shard_map/ppermute | solution.py:205
  590.9 18.2 %collective-permute-done.26 = bf16[512,1024]{1,0:T(8,128)(2,1)S(1)} collective-permute-done((bf16[512,1024]{1,0:T(8,128)(2,1)S(1)}, bf16[512,1024]{1,0:T(8,128)(2,1)S(1)}, u32[]{:S(2)}, u32[]{:S(2)}) %collective-permute-start.26) | collective-permute-done | bytes 1048608 | tf_op jit(solution)/shard_map/ppermute | solution.py:205
  612.3 16.8 %collective-permute-done.29 = bf16[512,1024]{1,0:T(8,128)(2,1)S(1)} collective-permute-done((bf16[512,1024]{1,0:T(8,128)(2,1)S(1)}, bf16[512,1024]{1,0:T(8,128)(2,1)S(1)}, u32[]{:S(2)}, u32[]{:S(2)}) %collective-permute-start.29) | collective-permute-done | bytes 1048608 | tf_op jit(solution)/shard_map/ppermute | solution.py:205
  (206 shorter events, 144.3 us)
Async XLA Ops:
  2.3 5.0 collective-permute-start
  11.3 39.0 %collective-permute-start.2 = (f32[9216]{0:T(1024)S(1)}, f32[9216]{0:T(1024)S(1)}, u32[]{:S(2)}, u32[]{:S(2)}) collective-permute-start(f32[9216]{0:T(1024)S(1)} %add.445), channel_id=1, source_target_pairs={{0,8},{2,10},{4,12},{6,14},{8,0},{10,2},{12,4},{14,6},{1,9},{3,11}... | collective-permute-start | bytes 110600 | tf_op jit(solution)/shard_map/ppermute | solution.py:112
  17.1 43.7 %collective-permute-start.11 = (bf16[512,1024]{1,0:T(8,128)(2,1)}, bf16[512,1024]{1,0:T(8,128)(2,1)}, u32[]{:S(2)}, u32[]{:S(2)}) collective-permute-start(bf16[512,1024]{1,0:T(8,128)(2,1)} %get-tuple-element.72), channel_id=1, source_target_pairs={{0,4},{4,8},{8,12},{12,14},{14,10},{10,6},{6,2},{2,0},{1,5},{5,9},... | collective-permute-start | bytes 3145736 | tf_op jit(solution)/shard_map/ppermute | solution.py:156
  18.7 97.0 %collective-permute-start.12 = (bf16[512,1024]{1,0:T(8,128)(2,1)}, bf16[512,1024]{1,0:T(8,128)(2,1)}, u32[]{:S(2)}, u32[]{:S(2)}) collective-permute-start(bf16[512,1024]{1,0:T(8,128)(2,1)} %get-tuple-element.72), channel_id=1, source_target_pairs={{4,0},{8,4},{12,8},{14,12},{10,14},{6,10},{2,6},{0,2},{5,1},{9,5},... | collective-permute-start | bytes 3145736 | tf_op jit(solution)/shard_map/ppermute | solution.py:156
  19.1 97.0 %collective-permute-start.5 = (bf16[512,1024]{1,0:T(8,128)(2,1)S(1)}, bf16[512,1024]{1,0:T(8,128)(2,1)}, u32[]{:S(2)}, u32[]{:S(2)}) collective-permute-start(bf16[512,1024]{1,0:T(8,128)(2,1)S(1)} %get-tuple-element.71), channel_id=1, source_target_pairs={{4,0},{8,4},{12,8},{14,12},{10,14},{6,10},{2,6},{0,2},{5,1},{9,5},... | collective-permute-start | bytes 3145736 | tf_op jit(solution)/shard_map/ppermute | solution.py:156
  20.7 107.9 %collective-permute-start.4 = (bf16[512,1024]{1,0:T(8,128)(2,1)S(1)}, bf16[512,1024]{1,0:T(8,128)(2,1)}, u32[]{:S(2)}, u32[]{:S(2)}) collective-permute-start(bf16[512,1024]{1,0:T(8,128)(2,1)S(1)} %get-tuple-element.71), channel_id=1, source_target_pairs={{0,4},{4,8},{8,12},{12,14},{14,10},{10,6},{6,2},{2,0},{1,5},{5,9},... | collective-permute-start | bytes 3145736 | tf_op jit(solution)/shard_map/ppermute | solution.py:156
  114.1 26.3 %collective-permute-start.13 = (bf16[512,1024]{1,0:T(8,128)(2,1)}, bf16[512,1024]{1,0:T(8,128)(2,1)}, u32[]{:S(2)}, u32[]{:S(2)}) collective-permute-start(bf16[512,1024]{1,0:T(8,128)(2,1)} %collective-permute-done.11), channel_id=1, source_target_pairs={{0,4},{4,8},{8,12},{12,14},{14,10},{10,6},{6,2},{2,0},{1,5},{5,9},... | collective-permute-start | bytes 3145736 | tf_op jit(solution)/shard_map/ppermute | solution.py:156
  115.7 79.6 %collective-permute-start.14 = (bf16[512,1024]{1,0:T(8,128)(2,1)}, bf16[512,1024]{1,0:T(8,128)(2,1)}, u32[]{:S(2)}, u32[]{:S(2)}) collective-permute-start(bf16[512,1024]{1,0:T(8,128)(2,1)} %collective-permute-done.12), channel_id=1, source_target_pairs={{4,0},{8,4},{12,8},{14,12},{10,14},{6,10},{2,6},{0,2},{5,1},{9,5},... | collective-permute-start | bytes 3145736 | tf_op jit(solution)/shard_map/ppermute | solution.py:156
  116.1 79.6 %collective-permute-start.7 = (bf16[512,1024]{1,0:T(8,128)(2,1)}, bf16[512,1024]{1,0:T(8,128)(2,1)}, u32[]{:S(2)}, u32[]{:S(2)}) collective-permute-start(bf16[512,1024]{1,0:T(8,128)(2,1)} %collective-permute-done.5), channel_id=1, source_target_pairs={{4,0},{8,4},{12,8},{14,12},{10,14},{6,10},{2,6},{0,2},{5,1},{9,5},... | collective-permute-start | bytes 3145736 | tf_op jit(solution)/shard_map/ppermute | solution.py:156
  128.6 79.6 %collective-permute-start.6 = (bf16[512,1024]{1,0:T(8,128)(2,1)}, bf16[512,1024]{1,0:T(8,128)(2,1)}, u32[]{:S(2)}, u32[]{:S(2)}) collective-permute-start(bf16[512,1024]{1,0:T(8,128)(2,1)} %collective-permute-done.4), channel_id=1, source_target_pairs={{0,4},{4,8},{8,12},{12,14},{14,10},{10,6},{6,2},{2,0},{1,5},{5,9},... | collective-permute-start | bytes 3145736 | tf_op jit(solution)/shard_map/ppermute | solution.py:156
  193.7 30.1 %collective-permute-start.15 = (bf16[512,1024]{1,0:T(8,128)(2,1)}, bf16[512,1024]{1,0:T(8,128)(2,1)}, u32[]{:S(2)}, u32[]{:S(2)}) collective-permute-start(bf16[512,1024]{1,0:T(8,128)(2,1)} %collective-permute-done.13), channel_id=1, source_target_pairs={{0,4},{4,8},{8,12},{12,14},{14,10},{10,6},{6,2},{2,0},{1,5},{5,9},... | collective-permute-start | bytes 3145736 | tf_op jit(solution)/shard_map/ppermute | solution.py:156
  195.3 161.1 %collective-permute-start.16 = (bf16[512,1024]{1,0:T(8,128)(2,1)}, bf16[512,1024]{1,0:T(8,128)(2,1)}, u32[]{:S(2)}, u32[]{:S(2)}) collective-permute-start(bf16[512,1024]{1,0:T(8,128)(2,1)} %collective-permute-done.14), channel_id=1, source_target_pairs={{4,0},{8,4},{12,8},{14,12},{10,14},{6,10},{2,6},{0,2},{5,1},{9,5},... | collective-permute-start | bytes 3145736 | tf_op jit(solution)/shard_map/ppermute | solution.py:156
  195.7 87.3 %collective-permute-start.9 = (bf16[512,1024]{1,0:T(8,128)(2,1)}, bf16[512,1024]{1,0:T(8,128)(2,1)}, u32[]{:S(2)}, u32[]{:S(2)}) collective-permute-start(bf16[512,1024]{1,0:T(8,128)(2,1)} %collective-permute-done.7), channel_id=1, source_target_pairs={{4,0},{8,4},{12,8},{14,12},{10,14},{6,10},{2,6},{0,2},{5,1},{9,5},... | collective-permute-start | bytes 3145736 | tf_op jit(solution)/shard_map/ppermute | solution.py:156
  208.1 86.0 %collective-permute-start.8 = (bf16[512,1024]{1,0:T(8,128)(2,1)}, bf16[512,1024]{1,0:T(8,128)(2,1)}, u32[]{:S(2)}, u32[]{:S(2)}) collective-permute-start(bf16[512,1024]{1,0:T(8,128)(2,1)} %collective-permute-done.6), channel_id=1, source_target_pairs={{0,4},{4,8},{8,12},{12,14},{14,10},{10,6},{6,2},{2,0},{1,5},{5,9},... | collective-permute-start | bytes 3145736 | tf_op jit(solution)/shard_map/ppermute | solution.py:156
  276.8 22.9 %collective-permute-start.17 = (bf16[512,1024]{1,0:T(8,128)(2,1)}, bf16[512,1024]{1,0:T(8,128)(2,1)}, u32[]{:S(2)}, u32[]{:S(2)}) collective-permute-start(bf16[512,1024]{1,0:T(8,128)(2,1)} %collective-permute-done.15), channel_id=1, source_target_pairs={{0,4},{4,8},{8,12},{12,14},{14,10},{10,6},{6,2},{2,0},{1,5},{5,9},... | collective-permute-start | bytes 3145736 | tf_op jit(solution)/shard_map/ppermute | solution.py:156
  283.0 84.7 %collective-permute-start.10 = (bf16[512,1024]{1,0:T(8,128)(2,1)}, bf16[512,1024]{1,0:T(8,128)(2,1)}, u32[]{:S(2)}, u32[]{:S(2)}) collective-permute-start(bf16[512,1024]{1,0:T(8,128)(2,1)} %collective-permute-done.9), channel_id=1, source_target_pairs={{4,0},{8,4},{12,8},{14,12},{10,14},{6,10},{2,6},{0,2},{5,1},{9,5},... | collective-permute-start | bytes 3145736 | tf_op jit(solution)/shard_map/ppermute | solution.py:156
  365.7 7.5 %collective-permute-start.18 = (bf16[512,1152]{1,0:T(8,128)(2,1)S(1)}, bf16[512,1152]{1,0:T(8,128)(2,1)S(1)}, u32[]{:S(2)}, u32[]{:S(2)}) collective-permute-start(bf16[512,1152]{1,0:T(8,128)(2,1)S(1)} %pad_maximum_fusion), channel_id=1, source_target_pairs={{0,1},{1,0},{2,3},{3,2},{4,5},{5,4},{6,7},{7,6},{8,9},{9,8},{10,11... | collective-permute-start | bytes 3538952 | tf_op jit(solution)/shard_map/ppermute | solution.py:169
  374.5 33.0 %all-to-all-start = ((bf16[8,64,1152]{2,1,0:T(8,128)(2,1)}), bf16[8,64,1152]{2,1,0:T(8,128)(2,1)S(1)}, u32[]{:S(2)}, u32[]{:S(2)}) async-start(bf16[8,64,1152]{2,1,0:T(8,128)(2,1)} %bitcast.94), calls=%async_computation | async-start | bytes 2359296 | tf_op jit(solution)/shard_map/all_to_all | solution.py:174
  460.5 53.8 %collective-permute-start.30 = (bf16[512,1024]{1,0:T(8,128)(2,1)S(1)}, bf16[512,1024]{1,0:T(8,128)(2,1)S(1)}, u32[]{:S(2)}, u32[]{:S(2)}) collective-permute-start(bf16[512,1024]{1,0:T(8,128)(2,1)S(1)} %convolution_convert_fusion), channel_id=1, source_target_pairs={{4,0},{8,4},{12,8},{14,12},{10,14},{6,10},{2,6},{0,2},{5,1},{9,5},... | collective-permute-start | bytes 3145736 | tf_op jit(solution)/shard_map/ppermute | solution.py:205
  463.3 75.5 %collective-permute-start.27 = (bf16[512,1024]{1,0:T(8,128)(2,1)S(1)}, bf16[512,1024]{1,0:T(8,128)(2,1)S(1)}, u32[]{:S(2)}, u32[]{:S(2)}) collective-permute-start(bf16[512,1024]{1,0:T(8,128)(2,1)S(1)} %convolution_convert_fusion.1), channel_id=1, source_target_pairs={{0,4},{4,8},{8,12},{12,14},{14,10},{10,6},{6,2},{2,0},{1,5},{5,9},... | collective-permute-start | bytes 3145736 | tf_op jit(solution)/shard_map/ppermute | solution.py:205
  465.2 45.9 %collective-permute-start.20 = (bf16[512,1024]{1,0:T(8,128)(2,1)S(1)}, bf16[512,1024]{1,0:T(8,128)(2,1)S(1)}, u32[]{:S(2)}, u32[]{:S(2)}) collective-permute-start(bf16[512,1024]{1,0:T(8,128)(2,1)S(1)} %convolution_convert_fusion.3), channel_id=1, source_target_pairs={{0,4},{4,8},{8,12},{12,14},{14,10},{10,6},{6,2},{2,0},{1,5},{5,9},... | collective-permute-start | bytes 3145736 | tf_op jit(solution)/shard_map/ppermute | solution.py:205
  470.7 46.3 %collective-permute-start.24 = (bf16[512,1024]{1,0:T(8,128)(2,1)S(1)}, bf16[512,1024]{1,0:T(8,128)(2,1)S(1)}, u32[]{:S(2)}, u32[]{:S(2)}) collective-permute-start(bf16[512,1024]{1,0:T(8,128)(2,1)S(1)} %convolution_convert_fusion.2), channel_id=1, source_target_pairs={{4,0},{8,4},{12,8},{14,12},{10,14},{6,10},{2,6},{0,2},{5,1},{9,5},... | collective-permute-start | bytes 3145736 | tf_op jit(solution)/shard_map/ppermute | solution.py:205
  512.4 24.5 %collective-permute-start.21 = (bf16[512,1024]{1,0:T(8,128)(2,1)S(1)}, bf16[512,1024]{1,0:T(8,128)(2,1)S(1)}, u32[]{:S(2)}, u32[]{:S(2)}) collective-permute-start(bf16[512,1024]{1,0:T(8,128)(2,1)S(1)} %add_convert_fusion.10), channel_id=1, source_target_pairs={{0,4},{4,8},{8,12},{12,14},{14,10},{10,6},{6,2},{2,0},{1,5},{5,9},... | collective-permute-start | bytes 3145736 | tf_op jit(solution)/shard_map/ppermute | solution.py:205
  515.5 26.1 %collective-permute-start.31 = (bf16[512,1024]{1,0:T(8,128)(2,1)S(1)}, bf16[512,1024]{1,0:T(8,128)(2,1)S(1)}, u32[]{:S(2)}, u32[]{:S(2)}) collective-permute-start(bf16[512,1024]{1,0:T(8,128)(2,1)S(1)} %add_convert_fusion.3), channel_id=1, source_target_pairs={{4,0},{8,4},{12,8},{14,12},{10,14},{6,10},{2,6},{0,2},{5,1},{9,5},... | collective-permute-start | bytes 3145736 | tf_op jit(solution)/shard_map/ppermute | solution.py:205
  518.3 45.8 %collective-permute-start.25 = (bf16[512,1024]{1,0:T(8,128)(2,1)S(1)}, bf16[512,1024]{1,0:T(8,128)(2,1)S(1)}, u32[]{:S(2)}, u32[]{:S(2)}) collective-permute-start(bf16[512,1024]{1,0:T(8,128)(2,1)S(1)} %add_convert_fusion.7), channel_id=1, source_target_pairs={{4,0},{8,4},{12,8},{14,12},{10,14},{6,10},{2,6},{0,2},{5,1},{9,5},... | collective-permute-start | bytes 3145736 | tf_op jit(solution)/shard_map/ppermute | solution.py:205
  538.2 28.8 %collective-permute-start.22 = (bf16[512,1024]{1,0:T(8,128)(2,1)S(1)}, bf16[512,1024]{1,0:T(8,128)(2,1)S(1)}, u32[]{:S(2)}, u32[]{:S(2)}) collective-permute-start(bf16[512,1024]{1,0:T(8,128)(2,1)S(1)} %add_convert_fusion.9), channel_id=1, source_target_pairs={{0,4},{4,8},{8,12},{12,14},{14,10},{10,6},{6,2},{2,0},{1,5},{5,9},... | collective-permute-start | bytes 3145736 | tf_op jit(solution)/shard_map/ppermute | solution.py:205
  540.1 46.7 %collective-permute-start.28 = (bf16[512,1024]{1,0:T(8,128)(2,1)S(1)}, bf16[512,1024]{1,0:T(8,128)(2,1)S(1)}, u32[]{:S(2)}, u32[]{:S(2)}) collective-permute-start(bf16[512,1024]{1,0:T(8,128)(2,1)S(1)} %add_convert_fusion.5), channel_id=1, source_target_pairs={{0,4},{4,8},{8,12},{12,14},{14,10},{10,6},{6,2},{2,0},{1,5},{5,9},... | collective-permute-start | bytes 3145736 | tf_op jit(solution)/shard_map/ppermute | solution.py:205
  542.1 45.7 %collective-permute-start.32 = (bf16[512,1024]{1,0:T(8,128)(2,1)S(1)}, bf16[512,1024]{1,0:T(8,128)(2,1)S(1)}, u32[]{:S(2)}, u32[]{:S(2)}) collective-permute-start(bf16[512,1024]{1,0:T(8,128)(2,1)S(1)} %add_convert_fusion.2), channel_id=1, source_target_pairs={{4,0},{8,4},{12,8},{14,12},{10,14},{6,10},{2,6},{0,2},{5,1},{9,5},... | collective-permute-start | bytes 3145736 | tf_op jit(solution)/shard_map/ppermute | solution.py:205
  565.4 43.7 %collective-permute-start.26 = (bf16[512,1024]{1,0:T(8,128)(2,1)S(1)}, bf16[512,1024]{1,0:T(8,128)(2,1)S(1)}, u32[]{:S(2)}, u32[]{:S(2)}) collective-permute-start(bf16[512,1024]{1,0:T(8,128)(2,1)S(1)} %add_convert_fusion.6), channel_id=1, source_target_pairs={{4,0},{8,4},{12,8},{14,12},{10,14},{6,10},{2,6},{0,2},{5,1},{9,5},... | collective-permute-start | bytes 3145736 | tf_op jit(solution)/shard_map/ppermute | solution.py:205
  568.2 41.0 %collective-permute-start.23 = (bf16[512,1024]{1,0:T(8,128)(2,1)S(1)}, bf16[512,1024]{1,0:T(8,128)(2,1)S(1)}, u32[]{:S(2)}, u32[]{:S(2)}) collective-permute-start(bf16[512,1024]{1,0:T(8,128)(2,1)S(1)} %add_convert_fusion.8), channel_id=1, source_target_pairs={{0,4},{4,8},{8,12},{12,14},{14,10},{10,6},{6,2},{2,0},{1,5},{5,9},... | collective-permute-start | bytes 3145736 | tf_op jit(solution)/shard_map/ppermute | solution.py:205
  587.2 42.0 %collective-permute-start.29 = (bf16[512,1024]{1,0:T(8,128)(2,1)S(1)}, bf16[512,1024]{1,0:T(8,128)(2,1)S(1)}, u32[]{:S(2)}, u32[]{:S(2)}) collective-permute-start(bf16[512,1024]{1,0:T(8,128)(2,1)S(1)} %add_convert_fusion.4), channel_id=1, source_target_pairs={{0,4},{4,8},{8,12},{12,14},{14,10},{10,6},{6,2},{2,0},{1,5},{5,9},... | collective-permute-start | bytes 3145736 | tf_op jit(solution)/shard_map/ppermute | solution.py:205
  588.2 41.5 %collective-permute-start.33 = (bf16[512,1024]{1,0:T(8,128)(2,1)S(1)}, bf16[512,1024]{1,0:T(8,128)(2,1)S(1)}, u32[]{:S(2)}, u32[]{:S(2)}) collective-permute-start(bf16[512,1024]{1,0:T(8,128)(2,1)S(1)} %add_convert_fusion.1), channel_id=1, source_target_pairs={{4,0},{8,4},{12,8},{14,12},{10,14},{6,10},{2,6},{0,2},{5,1},{9,5},... | collective-permute-start | bytes 3145736 | tf_op jit(solution)/shard_map/ppermute | solution.py:205
  (32 other events, 334.0 us)

commit v3 on v2

--- a/solution.py
+++ b/solution.py
@@ -115,6 +115,10 @@
         both = lax.psum(both, "gx")
     squares = both[:row_count]
     squares = squares + lax.ppermute(squares, "gy", [(0, 1), (1, 0)])
+    output_cols = w_output.reshape(w_output.shape[0], size, w_output.shape[3])
+    out_blocks, squares = lax.optimization_barrier(
+        (jnp.transpose(output_cols, (1, 0, 2)), squares)
+    )
     norm_scale = lax.rsqrt(squares / MODEL_WIDTH + epsilon)
     gain_mine = both[row_count:]
     scale_halves = [half_of(norm_scale, 0), half_of(norm_scale, 1)]
@@ -138,17 +142,6 @@
         old = sums[half]
         sums[half] = pair if old is None else (old[0] + pair[0], old[1] + pair[1])
 
-    out_blocks = {}
-
-    def load_block(offset, after):
-        weight, after = lax.optimization_barrier((w_output, after))
-        block = lax.dynamic_index_in_dim(weight[:, 0], at_place(offset), 1, keepdims=False)
-        block, after = lax.optimization_barrier((block, after))
-        out_blocks[offset % size] = block
-        return after
-
-    offsets = list(range(size))
-    per_step = -(-size // long_way)
     for step in range(1, long_way + 1):
         arrived = {}
         for chain in chains:
@@ -157,9 +150,6 @@
         if step == 1:
             for half in (0, 1):
                 add_to(half, project(state_halves[half], half, me))
-        for offset in offsets[(step - 1) * per_step : step * per_step]:
-            held_first = chains[0] if chains[0] in arrived else chains[1]
-            arrived[held_first] = load_block(offset, arrived[held_first])
         for chain, raw in arrived.items():
             add_to(chain[1], project(raw, chain[1], at_place(-chain[0] * step)))
         held.update(arrived)
@@ -191,9 +181,8 @@
     head_rows = [other_rows, own_rows]
 
     def term(half, dest):
-        return jnp.dot(
-            head_rows[half], out_blocks[dest % size], preferred_element_type=jnp.float32
-        )
+        block = lax.dynamic_index_in_dim(out_blocks, at_place(dest), 0, keepdims=False)
+        return jnp.dot(head_rows[half], block, preferred_element_type=jnp.float32)
 
     moving = {}
     for step in range(long_way, 0, -1):

time: 640 us -> 457 us (0.71)
  local copies, waits for them, and re-layouts: 227 us -> 28.9 us
  waiting for transfers between devices: 167 us -> 196 us
  matrix products: 125 us -> 116 us
    optimization_barrier x8 -> x0, local copies, waits for them, and re-layouts: 201 us -> none  [load_block(): weight, after = lax.optimization_barrier((w_output, after))]
    ppermute x14, waiting for transfers between devices: 1.6 us -> 64.2 us  [shards(): arrived[chain] = lax.ppermute(held[chain], 'gx', hops[chain[0]])]
    ppermute x14, waiting for transfers between devices: 132 us -> 96.5 us  [shards(): lax.ppermute(value.astype(jnp.bfloat16), 'gx', hops[chain[0]])]
    dot_general x16, matrix products: 21.7 us -> 47.6 us  [term(): return jnp.dot(head_rows[half], block, preferred_element_type=jnp.float32)]
    dot_general x16, matrix products: 66.4 us -> 40.5 us  [project(): jnp.dot(normed, wq, preferred_element_type=jnp.float32)]
    unnamed x58 -> x41, local copies, waits for them, and re-layouts: 2.12 us -> 19.1 us
    squeeze x8 -> x0, local copies, waits for them, and re-layouts: 12.2 us -> none  [load_block(): lax.dynamic_index_in_dim(weight[:, 0], at_place(offset), 1, keepdims=False)]
    dot_general x16, matrix products: 29 us -> 21.5 us  [project(): jnp.dot(normed, wkv, preferred_element_type=jnp.float32)]
  transfers between devices with their start and end apart: 35 -> 35, of which waited for: 15 -> 18; matrix products, arithmetic and copies ran while one was open for 53% -> 28% of each run, Pallas kernels for 0% -> 0%
where the time goes in v3:
time: 457 us; the launch traced here: 449 us
  waiting for transfers between devices  196 us (43%)
  matrix products  116 us (25%)
  starting transfers between devices  42 us (9%)
  between operations  29.6 us (6%)
  blocking collectives  29.4 us (6%)
  local copies, waits for them, and re-layouts  28.9 us (6%)
  other arithmetic  6.91 us (2%)
    ppermute x14, waiting for transfers between devices, shards(): lax.ppermute(value.astype(jnp.bfloat16), 'gx', hops[chain[0]])  96.5 us
    ppermute x14, waiting for transfers between devices, shards(): arrived[chain] = lax.ppermute(held[chain], 'gx', hops[chain[0]])  64.2 us
    dot_general x16, matrix products, term(): return jnp.dot(head_rows[half], block, preferred_element_type=jnp.float32)  47.6 us
    dot_general x16, matrix products, project(): jnp.dot(normed, wq, preferred_element_type=jnp.float32)  40.5 us
    all_to_all x1, blocking collectives, shards(): lax.all_to_all(attended, 'gx', split_axis=1, concat_axis=0, tiled=True)  29.4 us
    all_to_all x1, waiting for transfers between devices, shards(): lax.all_to_all(mine.reshape(size, rows_here, mine.shape[1]), 'gx', split_...  29.1 us
    dot_general x16, matrix products, project(): jnp.dot(normed, wkv, preferred_element_type=jnp.float32)  21.5 us
    unnamed x41, local copies, waits for them, and re-layouts  19.1 us
  transfers between devices with their start and end apart: 35, of which 18 were waited for; matrix products, arithmetic and copies ran while one was open for 28% of the time, Pallas kernels for 0%

profile of v3, /device:TPU:0, one launch (start us, length us, event | category | flops | bytes accessed | tf_op | source)
XLA Modules:
  0.0 448.9 jit_solution(2217102070723816469)
XLA Ops:
  11.3 3.1 collective-permute-start.2
  33.5 18.7 %copy.89 = bf16[1024,1,8,1024]{3,0,2,1:T(8,128)(2,1)} copy(bf16[1024,1,8,1024]{3,2,1,0:T(8,128)(2,1)} %param.14) | data formatting | bytes 33554432 | tf_op args[4]
  55.9 3.4 fusion.87
  59.3 3.0 fusion.89
  69.6 3.2 fusion.79
  84.7 3.9 collective-permute-done.14
  90.7 20.4 %collective-permute-done.7 = bf16[512,1024]{1,0:T(8,128)(2,1)S(1)} collective-permute-done((bf16[512,1024]{1,0:T(8,128)(2,1)}, bf16[512,1024]{1,0:T(8,128)(2,1)S(1)}, u32[]{:S(2)}, u32[]{:S(2)}) %collective-permute-start.7) | collective-permute-done | bytes 1048608 | tf_op jit(solution)/shard_map/ppermute | solution.py:149
  121.2 14.0 %collective-permute-done.15 = bf16[512,1024]{1,0:T(8,128)(2,1)} collective-permute-done((bf16[512,1024]{1,0:T(8,128)(2,1)S(1)}, bf16[512,1024]{1,0:T(8,128)(2,1)}, u32[]{:S(2)}, u32[]{:S(2)}) %collective-permute-start.15) | collective-permute-done | bytes 1048608 | tf_op jit(solution)/shard_map/ppermute | solution.py:149
  137.6 17.8 %collective-permute-done.9 = bf16[512,1024]{1,0:T(8,128)(2,1)} collective-permute-done((bf16[512,1024]{1,0:T(8,128)(2,1)S(1)}, bf16[512,1024]{1,0:T(8,128)(2,1)}, u32[]{:S(2)}, u32[]{:S(2)}) %collective-permute-start.9) | collective-permute-done | bytes 1048608 | tf_op jit(solution)/shard_map/ppermute | solution.py:149
  162.1 3.9 fusion.67
  171.0 8.0 %collective-permute-done.17 = bf16[512,1024]{1,0:T(8,128)(2,1)} collective-permute-done((bf16[512,1024]{1,0:T(8,128)(2,1)}, bf16[512,1024]{1,0:T(8,128)(2,1)}, u32[]{:S(2)}, u32[]{:S(2)}) %collective-permute-start.17) | collective-permute-done | bytes 1048608 | tf_op jit(solution)/shard_map/ppermute | solution.py:149
  179.1 4.4 add_convert_fusion.12
  187.7 3.3 add_convert_fusion.13
  192.4 3.7 all-to-all-start
  196.4 29.1 %all-to-all-done = bf16[8,64,1152]{2,1,0:T(8,128)(2,1)S(1)} async-done(((bf16[8,64,1152]{2,1,0:T(8,128)(2,1)}), bf16[8,64,1152]{2,1,0:T(8,128)(2,1)S(1)}, u32[]{:S(2)}, u32[]{:S(2)}) %all-to-all-start) | async-done | bytes 1179680 | tf_op jit(solution)/shard_map/all_to_all | solution.py:164
  236.6 3.4 divide_convert_fusion
  241.1 29.4 %all_to_all.24 = bf16[64,8,1024]{2,0,1:T(8,128)(2,1)S(1)} all-to-all(bf16[64,8,1024]{2,0,1:T(8,128)(2,1)S(1)} %copy.65), channel_id=1, replica_groups=mesh['groups'=2,'gx'=8,'gy'=2] {'gx'}, dimensions={1} | all-to-all | bytes 2097152 | tf_op jit(solution)/shard_map/all_to_all | solution.py:179
  273.2 3.8 fusion.94
  288.2 3.8 fusion.97
  293.4 9.1 %collective-permute-done.20 = bf16[512,1024]{1,0:T(8,128)(2,1)} collective-permute-done((bf16[512,1024]{1,0:T(8,128)(2,1)}, bf16[512,1024]{1,0:T(8,128)(2,1)}, u32[]{:S(2)}, u32[]{:S(2)}) %collective-permute-start.20) | collective-permute-done | bytes 1048608 | tf_op jit(solution)/shard_map/ppermute | solution.py:194
  302.6 4.1 add_convert_fusion.10
  319.1 3.4 add_convert_fusion.3
  323.8 8.1 %collective-permute-done.24 = bf16[512,1024]{1,0:T(8,128)(2,1)} collective-permute-done((bf16[512,1024]{1,0:T(8,128)(2,1)}, bf16[512,1024]{1,0:T(8,128)(2,1)}, u32[]{:S(2)}, u32[]{:S(2)}) %collective-permute-start.24) | collective-permute-done | bytes 1048608 | tf_op jit(solution)/shard_map/ppermute | solution.py:194
  331.9 3.1 add_convert_fusion.7
  336.0 3.4 add_convert_fusion.9
  340.3 15.2 %collective-permute-done.27 = bf16[512,1024]{1,0:T(8,128)(2,1)S(1)} collective-permute-done((bf16[512,1024]{1,0:T(8,128)(2,1)S(1)}, bf16[512,1024]{1,0:T(8,128)(2,1)S(1)}, u32[]{:S(2)}, u32[]{:S(2)}) %collective-permute-start.27) | collective-permute-done | bytes 1048608 | tf_op jit(solution)/shard_map/ppermute | solution.py:194
  360.2 16.6 %collective-permute-done.25 = bf16[512,1024]{1,0:T(8,128)(2,1)S(1)} collective-permute-done((bf16[512,1024]{1,0:T(8,128)(2,1)S(1)}, bf16[512,1024]{1,0:T(8,128)(2,1)S(1)}, u32[]{:S(2)}, u32[]{:S(2)}) %collective-permute-start.25) | collective-permute-done | bytes 1048608 | tf_op jit(solution)/shard_map/ppermute | solution.py:194
  383.3 17.1 %collective-permute-done.28 = bf16[512,1024]{1,0:T(8,128)(2,1)S(1)} collective-permute-done((bf16[512,1024]{1,0:T(8,128)(2,1)S(1)}, bf16[512,1024]{1,0:T(8,128)(2,1)S(1)}, u32[]{:S(2)}, u32[]{:S(2)}) %collective-permute-start.28) | collective-permute-done | bytes 1048608 | tf_op jit(solution)/shard_map/ppermute | solution.py:194
  409.3 12.4 %collective-permute-done.26 = bf16[512,1024]{1,0:T(8,128)(2,1)S(1)} collective-permute-done((bf16[512,1024]{1,0:T(8,128)(2,1)}, bf16[512,1024]{1,0:T(8,128)(2,1)S(1)}, u32[]{:S(2)}, u32[]{:S(2)}) %collective-permute-start.26) | collective-permute-done | bytes 1048608 | tf_op jit(solution)/shard_map/ppermute | solution.py:194
  423.2 3.7 fusion.137
  427.0 16.8 %collective-permute-done.29 = bf16[512,1024]{1,0:T(8,128)(2,1)} collective-permute-done((bf16[512,1024]{1,0:T(8,128)(2,1)}, bf16[512,1024]{1,0:T(8,128)(2,1)}, u32[]{:S(2)}, u32[]{:S(2)}) %collective-permute-start.29) | collective-permute-done | bytes 1048608 | tf_op jit(solution)/shard_map/ppermute | solution.py:194
  443.7 4.7 %fusion.142 = bf16[1024,1024]{1,0:T(8,128)(2,1)} fusion(bf16[1024,1024]{1,0:T(8,128)(2,1)} %copy-done.3, s32[]{:T(128)S(6)} %select_n.90, bf16[512,1024]{1,0:T(8,128)(2,1)} %collective-permute-done.33, bf16[512,1024]{1,0:T(8,128)(2,1)} %collective-permute-done.29, bf16[512,1024]{1,0:T(8,128)(2,1)S(1)} %bitcast.170, bf16[8,1024,1024]{2,1,0:T(8,128)(2,1)} %bitcast.145, ...), kind=kOutput, calls=%fused_computation.153 | convolution fusion | flops 1077411840 | bytes 7340040 | tf_op jit(solution)/shard_map/dot_general | solution.py:185
  (172 shorter events, 121.3 us)
Async XLA Ops:
  2.3 5.0 %collective-permute-start = (f32[9216]{0:T(1024)S(1)}, f32[9216]{0:T(1024)S(1)}, u32[]{:S(2)}, u32[]{:S(2)}) collective-permute-start(f32[9216]{0:T(1024)S(1)} %pad_maximum_fusion.4), channel_id=1, source_target_pairs={{0,2},{2,0},{4,6},{6,4},{8,10},{10,8},{12,14},{14,12},{1,3},{3,1},... | collective-permute-start | bytes 110600 | tf_op jit(solution)/shard_map/ppermute | solution.py:112
  11.3 40.9 %collective-permute-start.2 = (f32[9216]{0:T(1024)S(1)}, f32[9216]{0:T(1024)S(1)}, u32[]{:S(2)}, u32[]{:S(2)}) collective-permute-start(f32[9216]{0:T(1024)S(1)} %add.451), channel_id=1, source_target_pairs={{0,8},{2,10},{4,12},{6,14},{8,0},{10,2},{12,4},{14,6},{1,9},{3,11}... | collective-permute-start | bytes 110600 | tf_op jit(solution)/shard_map/ppermute | solution.py:112
  17.1 45.2 %collective-permute-start.12 = (bf16[512,1024]{1,0:T(8,128)(2,1)}, bf16[512,1024]{1,0:T(8,128)(2,1)}, u32[]{:S(2)}, u32[]{:S(2)}) collective-permute-start(bf16[512,1024]{1,0:T(8,128)(2,1)} %get-tuple-element.12), channel_id=1, source_target_pairs={{4,0},{8,4},{12,8},{14,12},{10,14},{6,10},{2,6},{0,2},{5,1},{9,5},... | collective-permute-start | bytes 3145736 | tf_op jit(solution)/shard_map/ppermute | solution.py:149
  18.6 45.3 %collective-permute-start.11 = (bf16[512,1024]{1,0:T(8,128)(2,1)}, bf16[512,1024]{1,0:T(8,128)(2,1)}, u32[]{:S(2)}, u32[]{:S(2)}) collective-permute-start(bf16[512,1024]{1,0:T(8,128)(2,1)} %get-tuple-element.12), channel_id=1, source_target_pairs={{0,4},{4,8},{8,12},{12,14},{14,10},{10,6},{6,2},{2,0},{1,5},{5,9},... | collective-permute-start | bytes 3145736 | tf_op jit(solution)/shard_map/ppermute | solution.py:149
  19.1 45.3 %collective-permute-start.5 = (bf16[512,1024]{1,0:T(8,128)(2,1)S(1)}, bf16[512,1024]{1,0:T(8,128)(2,1)}, u32[]{:S(2)}, u32[]{:S(2)}) collective-permute-start(bf16[512,1024]{1,0:T(8,128)(2,1)S(1)} %get-tuple-element.11), channel_id=1, source_target_pairs={{4,0},{8,4},{12,8},{14,12},{10,14},{6,10},{2,6},{0,2},{5,1},{9,5},... | collective-permute-start | bytes 3145736 | tf_op jit(solution)/shard_map/ppermute | solution.py:149
  20.7 54.7 %collective-permute-start.4 = (bf16[512,1024]{1,0:T(8,128)(2,1)S(1)}, bf16[512,1024]{1,0:T(8,128)(2,1)}, u32[]{:S(2)}, u32[]{:S(2)}) collective-permute-start(bf16[512,1024]{1,0:T(8,128)(2,1)S(1)} %get-tuple-element.11), channel_id=1, source_target_pairs={{0,4},{4,8},{8,12},{12,14},{14,10},{10,6},{6,2},{2,0},{1,5},{5,9},... | collective-permute-start | bytes 3145736 | tf_op jit(solution)/shard_map/ppermute | solution.py:149
  62.3 26.3 %collective-permute-start.14 = (bf16[512,1024]{1,0:T(8,128)(2,1)}, bf16[512,1024]{1,0:T(8,128)(2,1)S(1)}, u32[]{:S(2)}, u32[]{:S(2)}) collective-permute-start(bf16[512,1024]{1,0:T(8,128)(2,1)} %collective-permute-done.12), channel_id=1, source_target_pairs={{4,0},{8,4},{12,8},{14,12},{10,14},{6,10},{2,6},{0,2},{5,1},{9,5},... | collective-permute-start | bytes 3145736 | tf_op jit(solution)/shard_map/ppermute | solution.py:149
  63.9 26.3 %collective-permute-start.13 = (bf16[512,1024]{1,0:T(8,128)(2,1)}, bf16[512,1024]{1,0:T(8,128)(2,1)S(1)}, u32[]{:S(2)}, u32[]{:S(2)}) collective-permute-start(bf16[512,1024]{1,0:T(8,128)(2,1)} %collective-permute-done.11), channel_id=1, source_target_pairs={{0,4},{4,8},{8,12},{12,14},{14,10},{10,6},{6,2},{2,0},{1,5},{5,9},... | collective-permute-start | bytes 3145736 | tf_op jit(solution)/shard_map/ppermute | solution.py:149
  64.4 46.7 %collective-permute-start.7 = (bf16[512,1024]{1,0:T(8,128)(2,1)}, bf16[512,1024]{1,0:T(8,128)(2,1)S(1)}, u32[]{:S(2)}, u32[]{:S(2)}) collective-permute-start(bf16[512,1024]{1,0:T(8,128)(2,1)} %collective-permute-done.5), channel_id=1, source_target_pairs={{4,0},{8,4},{12,8},{14,12},{10,14},{6,10},{2,6},{0,2},{5,1},{9,5},... | collective-permute-start | bytes 3145736 | tf_op jit(solution)/shard_map/ppermute | solution.py:149
  75.4 40.4 %collective-permute-start.6 = (bf16[512,1024]{1,0:T(8,128)(2,1)}, bf16[512,1024]{1,0:T(8,128)(2,1)S(1)}, u32[]{:S(2)}, u32[]{:S(2)}) collective-permute-start(bf16[512,1024]{1,0:T(8,128)(2,1)} %collective-permute-done.4), channel_id=1, source_target_pairs={{0,4},{4,8},{8,12},{12,14},{14,10},{10,6},{6,2},{2,0},{1,5},{5,9},... | collective-permute-start | bytes 3145736 | tf_op jit(solution)/shard_map/ppermute | solution.py:149
  88.6 47.1 %collective-permute-start.16 = (bf16[512,1024]{1,0:T(8,128)(2,1)S(1)}, bf16[512,1024]{1,0:T(8,128)(2,1)S(1)}, u32[]{:S(2)}, u32[]{:S(2)}) collective-permute-start(bf16[512,1024]{1,0:T(8,128)(2,1)S(1)} %collective-permute-done.14), channel_id=1, source_target_pairs={{4,0},{8,4},{12,8},{14,12},{10,14},{6,10},{2,6},{0,2},{5,1},{9,5},... | collective-permute-start | bytes 3145736 | tf_op jit(solution)/shard_map/ppermute | solution.py:149
  90.2 45.0 %collective-permute-start.15 = (bf16[512,1024]{1,0:T(8,128)(2,1)S(1)}, bf16[512,1024]{1,0:T(8,128)(2,1)}, u32[]{:S(2)}, u32[]{:S(2)}) collective-permute-start(bf16[512,1024]{1,0:T(8,128)(2,1)S(1)} %collective-permute-done.13), channel_id=1, source_target_pairs={{0,4},{4,8},{8,12},{12,14},{14,10},{10,6},{6,2},{2,0},{1,5},{5,9},... | collective-permute-start | bytes 3145736 | tf_op jit(solution)/shard_map/ppermute | solution.py:149
  111.1 44.3 %collective-permute-start.9 = (bf16[512,1024]{1,0:T(8,128)(2,1)S(1)}, bf16[512,1024]{1,0:T(8,128)(2,1)}, u32[]{:S(2)}, u32[]{:S(2)}) collective-permute-start(bf16[512,1024]{1,0:T(8,128)(2,1)S(1)} %collective-permute-done.7), channel_id=1, source_target_pairs={{4,0},{8,4},{12,8},{14,12},{10,14},{6,10},{2,6},{0,2},{5,1},{9,5},... | collective-permute-start | bytes 3145736 | tf_op jit(solution)/shard_map/ppermute | solution.py:149
  115.8 52.7 %collective-permute-start.8 = (bf16[512,1024]{1,0:T(8,128)(2,1)S(1)}, bf16[512,1024]{1,0:T(8,128)(2,1)}, u32[]{:S(2)}, u32[]{:S(2)}) collective-permute-start(bf16[512,1024]{1,0:T(8,128)(2,1)S(1)} %collective-permute-done.6), channel_id=1, source_target_pairs={{0,4},{4,8},{8,12},{12,14},{14,10},{10,6},{6,2},{2,0},{1,5},{5,9},... | collective-permute-start | bytes 3145736 | tf_op jit(solution)/shard_map/ppermute | solution.py:149
  135.2 43.8 %collective-permute-start.17 = (bf16[512,1024]{1,0:T(8,128)(2,1)}, bf16[512,1024]{1,0:T(8,128)(2,1)}, u32[]{:S(2)}, u32[]{:S(2)}) collective-permute-start(bf16[512,1024]{1,0:T(8,128)(2,1)} %collective-permute-done.15), channel_id=1, source_target_pairs={{0,4},{4,8},{8,12},{12,14},{14,10},{10,6},{6,2},{2,0},{1,5},{5,9},... | collective-permute-start | bytes 3145736 | tf_op jit(solution)/shard_map/ppermute | solution.py:149
  155.3 31.8 %collective-permute-start.10 = (bf16[512,1024]{1,0:T(8,128)(2,1)}, bf16[512,1024]{1,0:T(8,128)(2,1)S(1)}, u32[]{:S(2)}, u32[]{:S(2)}) collective-permute-start(bf16[512,1024]{1,0:T(8,128)(2,1)} %collective-permute-done.9), channel_id=1, source_target_pairs={{4,0},{8,4},{12,8},{14,12},{10,14},{6,10},{2,6},{0,2},{5,1},{9,5},... | collective-permute-start | bytes 3145736 | tf_op jit(solution)/shard_map/ppermute | solution.py:149
  185.4 5.7 %collective-permute-start.18 = (bf16[512,1152]{1,0:T(8,128)(2,1)S(1)}, bf16[512,1152]{1,0:T(8,128)(2,1)S(1)}, u32[]{:S(2)}, u32[]{:S(2)}) collective-permute-start(bf16[512,1152]{1,0:T(8,128)(2,1)S(1)} %pad_maximum_fusion), channel_id=1, source_target_pairs={{0,1},{1,0},{2,3},{3,2},{4,5},{5,4},{6,7},{7,6},{8,9},{9,8},{10,11... | collective-permute-start | bytes 3538952 | tf_op jit(solution)/shard_map/ppermute | solution.py:159
  192.4 33.2 %all-to-all-start = ((bf16[8,64,1152]{2,1,0:T(8,128)(2,1)}), bf16[8,64,1152]{2,1,0:T(8,128)(2,1)S(1)}, u32[]{:S(2)}, u32[]{:S(2)}) async-start(bf16[8,64,1152]{2,1,0:T(8,128)(2,1)} %bitcast.18), calls=%async_computation | async-start | bytes 2359296 | tf_op jit(solution)/shard_map/all_to_all | solution.py:164
  277.0 25.5 %collective-permute-start.20 = (bf16[512,1024]{1,0:T(8,128)(2,1)}, bf16[512,1024]{1,0:T(8,128)(2,1)}, u32[]{:S(2)}, u32[]{:S(2)}) collective-permute-start(bf16[512,1024]{1,0:T(8,128)(2,1)} %fusion.94), channel_id=1, source_target_pairs={{0,4},{4,8},{8,12},{12,14},{14,10},{10,6},{6,2},{2,0},{1,5},{5,9},... | collective-permute-start | bytes 3145736 | tf_op jit(solution)/shard_map/ppermute | solution.py:194
  283.0 36.1 %collective-permute-start.30 = (bf16[512,1024]{1,0:T(8,128)(2,1)S(1)}, bf16[512,1024]{1,0:T(8,128)(2,1)}, u32[]{:S(2)}, u32[]{:S(2)}) collective-permute-start(bf16[512,1024]{1,0:T(8,128)(2,1)S(1)} %fusion.100), channel_id=1, source_target_pairs={{4,0},{8,4},{12,8},{14,12},{10,14},{6,10},{2,6},{0,2},{5,1},{9,5},... | collective-permute-start | bytes 3145736 | tf_op jit(solution)/shard_map/ppermute | solution.py:194
  292.0 40.0 %collective-permute-start.24 = (bf16[512,1024]{1,0:T(8,128)(2,1)}, bf16[512,1024]{1,0:T(8,128)(2,1)}, u32[]{:S(2)}, u32[]{:S(2)}) collective-permute-start(bf16[512,1024]{1,0:T(8,128)(2,1)} %fusion.97), channel_id=1, source_target_pairs={{4,0},{8,4},{12,8},{14,12},{10,14},{6,10},{2,6},{0,2},{5,1},{9,5},... | collective-permute-start | bytes 3145736 | tf_op jit(solution)/shard_map/ppermute | solution.py:194
  306.7 29.3 %collective-permute-start.21 = (bf16[512,1024]{1,0:T(8,128)(2,1)}, bf16[512,1024]{1,0:T(8,128)(2,1)}, u32[]{:S(2)}, u32[]{:S(2)}) collective-permute-start(bf16[512,1024]{1,0:T(8,128)(2,1)} %add_convert_fusion.10), channel_id=1, source_target_pairs={{0,4},{4,8},{8,12},{12,14},{14,10},{10,6},{6,2},{2,0},{1,5},{5,9},... | collective-permute-start | bytes 3145736 | tf_op jit(solution)/shard_map/ppermute | solution.py:194
  318.5 37.0 %collective-permute-start.27 = (bf16[512,1024]{1,0:T(8,128)(2,1)S(1)}, bf16[512,1024]{1,0:T(8,128)(2,1)S(1)}, u32[]{:S(2)}, u32[]{:S(2)}) collective-permute-start(bf16[512,1024]{1,0:T(8,128)(2,1)S(1)} %fusion.91), channel_id=1, source_target_pairs={{0,4},{4,8},{8,12},{12,14},{14,10},{10,6},{6,2},{2,0},{1,5},{5,9},... | collective-permute-start | bytes 3145736 | tf_op jit(solution)/shard_map/ppermute | solution.py:194
  322.5 35.4 %collective-permute-start.31 = (bf16[512,1024]{1,0:T(8,128)(2,1)S(1)}, bf16[512,1024]{1,0:T(8,128)(2,1)S(1)}, u32[]{:S(2)}, u32[]{:S(2)}) collective-permute-start(bf16[512,1024]{1,0:T(8,128)(2,1)S(1)} %add_convert_fusion.3), channel_id=1, source_target_pairs={{4,0},{8,4},{12,8},{14,12},{10,14},{6,10},{2,6},{0,2},{5,1},{9,5},... | collective-permute-start | bytes 3145736 | tf_op jit(solution)/shard_map/ppermute | solution.py:194
  335.0 41.7 %collective-permute-start.25 = (bf16[512,1024]{1,0:T(8,128)(2,1)S(1)}, bf16[512,1024]{1,0:T(8,128)(2,1)S(1)}, u32[]{:S(2)}, u32[]{:S(2)}) collective-permute-start(bf16[512,1024]{1,0:T(8,128)(2,1)S(1)} %add_convert_fusion.7), channel_id=1, source_target_pairs={{4,0},{8,4},{12,8},{14,12},{10,14},{6,10},{2,6},{0,2},{5,1},{9,5},... | collective-permute-start | bytes 3145736 | tf_op jit(solution)/shard_map/ppermute | solution.py:194
  339.4 40.5 %collective-permute-start.22 = (bf16[512,1024]{1,0:T(8,128)(2,1)S(1)}, bf16[512,1024]{1,0:T(8,128)(2,1)S(1)}, u32[]{:S(2)}, u32[]{:S(2)}) collective-permute-start(bf16[512,1024]{1,0:T(8,128)(2,1)S(1)} %add_convert_fusion.9), channel_id=1, source_target_pairs={{0,4},{4,8},{8,12},{12,14},{14,10},{10,6},{6,2},{2,0},{1,5},{5,9},... | collective-permute-start | bytes 3145736 | tf_op jit(solution)/shard_map/ppermute | solution.py:194
  356.8 43.6 %collective-permute-start.28 = (bf16[512,1024]{1,0:T(8,128)(2,1)S(1)}, bf16[512,1024]{1,0:T(8,128)(2,1)S(1)}, u32[]{:S(2)}, u32[]{:S(2)}) collective-permute-start(bf16[512,1024]{1,0:T(8,128)(2,1)S(1)} %add_convert_fusion.5), channel_id=1, source_target_pairs={{0,4},{4,8},{8,12},{12,14},{14,10},{10,6},{6,2},{2,0},{1,5},{5,9},... | collective-permute-start | bytes 3145736 | tf_op jit(solution)/shard_map/ppermute | solution.py:194
  359.2 44.8 %collective-permute-start.32 = (bf16[512,1024]{1,0:T(8,128)(2,1)S(1)}, bf16[512,1024]{1,0:T(8,128)(2,1)S(1)}, u32[]{:S(2)}, u32[]{:S(2)}) collective-permute-start(bf16[512,1024]{1,0:T(8,128)(2,1)S(1)} %add_convert_fusion.2), channel_id=1, source_target_pairs={{4,0},{8,4},{12,8},{14,12},{10,14},{6,10},{2,6},{0,2},{5,1},{9,5},... | collective-permute-start | bytes 3145736 | tf_op jit(solution)/shard_map/ppermute | solution.py:194
  379.0 42.7 %collective-permute-start.26 = (bf16[512,1024]{1,0:T(8,128)(2,1)}, bf16[512,1024]{1,0:T(8,128)(2,1)S(1)}, u32[]{:S(2)}, u32[]{:S(2)}) collective-permute-start(bf16[512,1024]{1,0:T(8,128)(2,1)} %add_convert_fusion.6), channel_id=1, source_target_pairs={{4,0},{8,4},{12,8},{14,12},{10,14},{6,10},{2,6},{0,2},{5,1},{9,5},... | collective-permute-start | bytes 3145736 | tf_op jit(solution)/shard_map/ppermute | solution.py:194
  382.2 40.8 %collective-permute-start.23 = (bf16[512,1024]{1,0:T(8,128)(2,1)}, bf16[512,1024]{1,0:T(8,128)(2,1)}, u32[]{:S(2)}, u32[]{:S(2)}) collective-permute-start(bf16[512,1024]{1,0:T(8,128)(2,1)} %add_convert_fusion.8), channel_id=1, source_target_pairs={{0,4},{4,8},{8,12},{12,14},{14,10},{10,6},{6,2},{2,0},{1,5},{5,9},... | collective-permute-start | bytes 3145736 | tf_op jit(solution)/shard_map/ppermute | solution.py:194
  402.7 41.1 %collective-permute-start.29 = (bf16[512,1024]{1,0:T(8,128)(2,1)}, bf16[512,1024]{1,0:T(8,128)(2,1)}, u32[]{:S(2)}, u32[]{:S(2)}) collective-permute-start(bf16[512,1024]{1,0:T(8,128)(2,1)} %add_convert_fusion.4), channel_id=1, source_target_pairs={{0,4},{4,8},{8,12},{12,14},{14,10},{10,6},{6,2},{2,0},{1,5},{5,9},... | collective-permute-start | bytes 3145736 | tf_op jit(solution)/shard_map/ppermute | solution.py:194
  406.3 37.4 %collective-permute-start.33 = (bf16[512,1024]{1,0:T(8,128)(2,1)}, bf16[512,1024]{1,0:T(8,128)(2,1)}, u32[]{:S(2)}, u32[]{:S(2)}) collective-permute-start(bf16[512,1024]{1,0:T(8,128)(2,1)} %add_convert_fusion.1), channel_id=1, source_target_pairs={{4,0},{8,4},{12,8},{14,12},{10,14},{6,10},{2,6},{0,2},{5,1},{9,5},... | collective-permute-start | bytes 3145736 | tf_op jit(solution)/shard_map/ppermute | solution.py:194
  (23 other events, 390.8 us)

commit v4 on v3

--- a/solution.py
+++ b/solution.py
@@ -168,17 +168,22 @@
     queries = spread[:, :, :query_width].reshape(rows_here, -1)
     keyvals = spread[:, :, query_width:].reshape(rows_here, -1)
     key_span_width = keyvals.shape[1] // 2
-    attended = attend(
-        queries,
-        keyvals[:, :key_span_width],
-        keyvals[:, key_span_width:],
-        key_cache,
-        cached_value_rows,
-        lengths,
-    )
-    own_rows = lax.all_to_all(attended, "gx", split_axis=1, concat_axis=0, tiled=True)
-    other_rows = lax.ppermute(own_rows, "gy", pair)
-    head_rows = [other_rows, own_rows]
+    part_rows = rows_here // 2
+    head_rows = []
+    for part in (0, 1):
+        span = slice(part * part_rows, (part + 1) * part_rows)
+        attended = attend(
+            queries[span],
+            keyvals[span, :key_span_width],
+            keyvals[span, key_span_width:],
+            key_cache[span],
+            cached_value_rows[span],
+            lengths[span],
+        )
+        own_rows = lax.all_to_all(attended, "gx", split_axis=1, concat_axis=0, tiled=True)
+        other_rows = lax.ppermute(own_rows, "gy", pair)
+        head_rows.append(jnp.concatenate([own_rows, other_rows], axis=0))
+    parted = states.reshape(2, size, 2, part_rows, width)
 
     def term(half, dest):
         block = lax.dynamic_index_in_dim(out_blocks, at_place(dest), 0, keepdims=False)
@@ -186,7 +191,7 @@
 
     moving = {}
     for step in range(long_way, 0, -1):
-        for chain in chains[2:] + chains[:2]:
+        for chain in chains:
             if step <= reach[chain]:
                 value = term(chain[1], chain[0] * step)
                 if chain in moving:
@@ -194,14 +199,14 @@
                 moving[chain] = lax.ppermute(value.astype(jnp.bfloat16), "gx", hops[chain[0]])
     halves = []
     for half in (0, 1):
-        total = state_halves[half].astype(jnp.float32) + term(half, 0)
+        total = term(half, 0)
         for chain in chains:
             if chain[1] == half and chain in moving:
                 total = total + moving[chain].astype(jnp.float32)
-        halves.append(total.astype(jnp.bfloat16))
-    out = jnp.zeros((row_count, width), jnp.bfloat16)
-    out = lax.dynamic_update_slice(out, halves[0], (other * half_rows, 0))
-    return lax.dynamic_update_slice(out, halves[1], (core * half_rows, 0))
+        total = total.reshape(2, size, part_rows, width)
+        total = jnp.where(core == 0, total, total[::-1])
+        halves.append((parted[:, :, half].astype(jnp.float32) + total).astype(jnp.bfloat16))
+    return jnp.stack(halves, axis=2).reshape(row_count, width)
 
 
 def solution(mesh):

time: 457 us -> 459 us (level)
  blocking collectives: 29.4 us -> 0 us
  matrix products: 116 us -> 134 us
  starting transfers between devices: 42 us -> 49.4 us
  other arithmetic: 6.91 us -> 11.9 us
    all_to_all x1 -> x0, blocking collectives: 29.4 us -> none  [shards(): lax.all_to_all(attended, 'gx', split_axis=1, concat_axis=0, tiled=True)]
    all_to_all x0 -> x2, waiting for transfers between devices: none -> 19 us  [shards(): lax.all_to_all(attended, 'gx', split_axis=1, concat_axis=0, tiled=True)]
    ppermute x14, waiting for transfers between devices: 96.5 us -> 78.6 us  [shards(): lax.ppermute(value.astype(jnp.bfloat16), 'gx', hops[chain[0]])]
    dot_general x16, matrix products: 47.6 us -> 61.3 us  [term(): return jnp.dot(head_rows[half], block, preferred_element_type=jnp.float32)]
    all_to_all x0 -> x2, starting transfers between devices: none -> 7.5 us  [shards(): lax.all_to_all(attended, 'gx', split_axis=1, concat_axis=0, tiled=True)]
    unnamed x41 -> x29, local copies, waits for them, and re-layouts: 19.1 us -> 19.8 us
  transfers between devices with their start and end apart: 35 -> 38, of which waited for: 18 -> 19; matrix products, arithmetic and copies ran while one was open for 28% -> 35% of each run, Pallas kernels for 0% -> 0%
where the time goes in v4:
time: 459 us; the launch traced here: 451 us
  waiting for transfers between devices  196 us (43%)
  matrix products  134 us (29%)
  starting transfers between devices  49.4 us (11%)
  local copies, waits for them, and re-layouts  31.9 us (7%)
  between operations  28 us (6%)
  other arithmetic  11.9 us (3%)
    ppermute x14, waiting for transfers between devices, shards(): lax.ppermute(value.astype(jnp.bfloat16), 'gx', hops[chain[0]])  78.6 us
    ppermute x14, waiting for transfers between devices, shards(): arrived[chain] = lax.ppermute(held[chain], 'gx', hops[chain[0]])  64.1 us
    dot_general x16, matrix products, term(): return jnp.dot(head_rows[half], block, preferred_element_type=jnp.float32)  61.3 us
    dot_general x16, matrix products, project(): jnp.dot(normed, wq, preferred_element_type=jnp.float32)  40.5 us
    all_to_all x1, waiting for transfers between devices, shards(): lax.all_to_all(mine.reshape(size, rows_here, mine.shape[1]), 'gx', split_...  29 us
    dot_general x16, matrix products, project(): jnp.dot(normed, wkv, preferred_element_type=jnp.float32)  21.5 us
    unnamed x29, local copies, waits for them, and re-layouts  19.8 us
    all_to_all x2, waiting for transfers between devices, shards(): lax.all_to_all(attended, 'gx', split_axis=1, concat_axis=0, tiled=True)  19 us
  transfers between devices with their start and end apart: 38, of which 19 were waited for; matrix products, arithmetic and copies ran while one was open for 35% of the time, Pallas kernels for 0%

profile of v4, /device:TPU:0, one launch (start us, length us, event | category | flops | bytes accessed | tf_op | source)
XLA Modules:
  0.0 450.5 jit_solution(4164515391027838443)
XLA Ops:
  32.5 18.7 %copy.107 = bf16[1024,1,8,1024]{3,0,2,1:T(8,128)(2,1)} copy(bf16[1024,1,8,1024]{3,2,1,0:T(8,128)(2,1)} %param.14) | data formatting | bytes 33554432 | tf_op args[4]
  83.7 3.9 collective-permute-done.14
  89.6 20.4 %collective-permute-done.7 = bf16[512,1024]{1,0:T(8,128)(2,1)S(1)} collective-permute-done((bf16[512,1024]{1,0:T(8,128)(2,1)}, bf16[512,1024]{1,0:T(8,128)(2,1)S(1)}, u32[]{:S(2)}, u32[]{:S(2)}) %collective-permute-start.7) | collective-permute-done | bytes 1048608 | tf_op jit(solution)/shard_map/ppermute | solution.py:149
  120.2 14.0 %collective-permute-done.15 = bf16[512,1024]{1,0:T(8,128)(2,1)} collective-permute-done((bf16[512,1024]{1,0:T(8,128)(2,1)S(1)}, bf16[512,1024]{1,0:T(8,128)(2,1)}, u32[]{:S(2)}, u32[]{:S(2)}) %collective-permute-start.15) | collective-permute-done | bytes 1048608 | tf_op jit(solution)/shard_map/ppermute | solution.py:149
  136.5 17.8 %collective-permute-done.9 = bf16[512,1024]{1,0:T(8,128)(2,1)} collective-permute-done((bf16[512,1024]{1,0:T(8,128)(2,1)S(1)}, bf16[512,1024]{1,0:T(8,128)(2,1)}, u32[]{:S(2)}, u32[]{:S(2)}) %collective-permute-start.9) | collective-permute-done | bytes 1048608 | tf_op jit(solution)/shard_map/ppermute | solution.py:149
  161.1 3.9 fusion.68
  170.0 8.0 %collective-permute-done.17 = bf16[512,1024]{1,0:T(8,128)(2,1)} collective-permute-done((bf16[512,1024]{1,0:T(8,128)(2,1)}, bf16[512,1024]{1,0:T(8,128)(2,1)}, u32[]{:S(2)}, u32[]{:S(2)}) %collective-permute-start.17) | collective-permute-done | bytes 1048608 | tf_op jit(solution)/shard_map/ppermute | solution.py:149
  178.0 4.4 add_convert_fusion.11
  191.4 3.7 all-to-all-start
  195.5 29.0 %all-to-all-done = bf16[8,64,1152]{2,1,0:T(8,128)(2,1)S(1)} async-done(((bf16[8,64,1152]{2,1,0:T(8,128)(2,1)}), bf16[8,64,1152]{2,1,0:T(8,128)(2,1)S(1)}, u32[]{:S(2)}, u32[]{:S(2)}) %all-to-all-start) | async-done | bytes 1179680 | tf_op jit(solution)/shard_map/all_to_all | solution.py:164
  236.9 3.6 all-to-all-start.1
  248.7 6.5 %all-to-all-done.1 = bf16[32,8,1024]{2,0,1:T(8,128)(2,1)S(1)} async-done(((bf16[32,8,1024]{2,0,1:T(8,128)(2,1)}), bf16[32,8,1024]{2,0,1:T(8,128)(2,1)S(1)}, u32[]{:S(2)}, u32[]{:S(2)}) %all-to-all-start.1) | async-done | bytes 524320 | tf_op jit(solution)/shard_map/all_to_all | solution.py:183
  255.2 3.9 all-to-all-start.2
  261.2 12.5 %all-to-all-done.2 = bf16[32,8,1024]{2,0,1:T(8,128)(2,1)S(1)} async-done(((bf16[32,8,1024]{2,0,1:T(8,128)(2,1)}), bf16[32,8,1024]{2,0,1:T(8,128)(2,1)S(1)}, u32[]{:S(2)}, u32[]{:S(2)}) %all-to-all-start.2) | async-done | bytes 524320 | tf_op jit(solution)/shard_map/all_to_all | solution.py:183
  273.7 3.8 fusion.95
  288.3 3.8 fusion.98
  293.6 9.8 %collective-permute-done.20 = bf16[512,1024]{1,0:T(8,128)(2,1)} collective-permute-done((bf16[512,1024]{1,0:T(8,128)(2,1)}, bf16[512,1024]{1,0:T(8,128)(2,1)}, u32[]{:S(2)}, u32[]{:S(2)}) %collective-permute-start.20) | collective-permute-done | bytes 1048608 | tf_op jit(solution)/shard_map/ppermute | solution.py:199
  303.4 4.1 add_convert_fusion.10
  308.3 4.0 fusion.92
  321.2 10.9 %collective-permute-done.24 = bf16[512,1024]{1,0:T(8,128)(2,1)} collective-permute-done((bf16[512,1024]{1,0:T(8,128)(2,1)}, bf16[512,1024]{1,0:T(8,128)(2,1)}, u32[]{:S(2)}, u32[]{:S(2)}) %collective-permute-start.24) | collective-permute-done | bytes 1048608 | tf_op jit(solution)/shard_map/ppermute | solution.py:199
  332.1 4.1 add_convert_fusion.7
  337.4 4.1 add_convert_fusion.9
  342.3 14.1 %collective-permute-done.28 = bf16[512,1024]{1,0:T(8,128)(2,1)} collective-permute-done((bf16[512,1024]{1,0:T(8,128)(2,1)}, bf16[512,1024]{1,0:T(8,128)(2,1)}, u32[]{:S(2)}, u32[]{:S(2)}) %collective-permute-start.28) | collective-permute-done | bytes 1048608 | tf_op jit(solution)/shard_map/ppermute | solution.py:199
  356.4 4.3 add_convert_fusion.5
  361.4 4.3 add_convert_fusion.2
  370.6 6.4 %collective-permute-done.25 = bf16[512,1024]{1,0:T(8,128)(2,1)} collective-permute-done((bf16[512,1024]{1,0:T(8,128)(2,1)}, bf16[512,1024]{1,0:T(8,128)(2,1)}, u32[]{:S(2)}, u32[]{:S(2)}) %collective-permute-start.25) | collective-permute-done | bytes 1048608 | tf_op jit(solution)/shard_map/ppermute | solution.py:199
  377.0 4.1 add_convert_fusion.6
  382.6 4.1 add_convert_fusion.8
  387.5 13.9 %collective-permute-done.29 = bf16[512,1024]{1,0:T(8,128)(2,1)} collective-permute-done((bf16[512,1024]{1,0:T(8,128)(2,1)}, bf16[512,1024]{1,0:T(8,128)(2,1)}, u32[]{:S(2)}, u32[]{:S(2)}) %collective-permute-start.29) | collective-permute-done | bytes 1048608 | tf_op jit(solution)/shard_map/ppermute | solution.py:199
  401.3 4.3 add_convert_fusion.4
  406.4 4.2 add_convert_fusion.1
  425.6 19.4 %collective-permute-done.30 = bf16[512,1024]{1,0:T(8,128)(2,1)} collective-permute-done((bf16[512,1024]{1,0:T(8,128)(2,1)}, bf16[512,1024]{1,0:T(8,128)(2,1)}, u32[]{:S(2)}, u32[]{:S(2)}) %collective-permute-start.30) | collective-permute-done | bytes 1048608 | tf_op jit(solution)/shard_map/ppermute | solution.py:199
  (182 shorter events, 148.7 us)
Async XLA Ops:
  11.3 39.8 %collective-permute-start.2 = (f32[9216]{0:T(1024)S(1)}, f32[9216]{0:T(1024)S(1)}, u32[]{:S(2)}, u32[]{:S(2)}) collective-permute-start(f32[9216]{0:T(1024)S(1)} %add.460), channel_id=1, source_target_pairs={{0,8},{2,10},{4,12},{6,14},{8,0},{10,2},{12,4},{14,6},{1,9},{3,11}... | collective-permute-start | bytes 110600 | tf_op jit(solution)/shard_map/ppermute | solution.py:112
  17.1 44.2 %collective-permute-start.12 = (bf16[512,1024]{1,0:T(8,128)(2,1)}, bf16[512,1024]{1,0:T(8,128)(2,1)}, u32[]{:S(2)}, u32[]{:S(2)}) collective-permute-start(bf16[512,1024]{1,0:T(8,128)(2,1)} %get-tuple-element.12), channel_id=1, source_target_pairs={{4,0},{8,4},{12,8},{14,12},{10,14},{6,10},{2,6},{0,2},{5,1},{9,5},... | collective-permute-start | bytes 3145736 | tf_op jit(solution)/shard_map/ppermute | solution.py:149
  18.6 44.3 %collective-permute-start.11 = (bf16[512,1024]{1,0:T(8,128)(2,1)}, bf16[512,1024]{1,0:T(8,128)(2,1)}, u32[]{:S(2)}, u32[]{:S(2)}) collective-permute-start(bf16[512,1024]{1,0:T(8,128)(2,1)} %get-tuple-element.12), channel_id=1, source_target_pairs={{0,4},{4,8},{8,12},{12,14},{14,10},{10,6},{6,2},{2,0},{1,5},{5,9},... | collective-permute-start | bytes 3145736 | tf_op jit(solution)/shard_map/ppermute | solution.py:149
  19.1 44.3 %collective-permute-start.5 = (bf16[512,1024]{1,0:T(8,128)(2,1)S(1)}, bf16[512,1024]{1,0:T(8,128)(2,1)}, u32[]{:S(2)}, u32[]{:S(2)}) collective-permute-start(bf16[512,1024]{1,0:T(8,128)(2,1)S(1)} %get-tuple-element.11), channel_id=1, source_target_pairs={{4,0},{8,4},{12,8},{14,12},{10,14},{6,10},{2,6},{0,2},{5,1},{9,5},... | collective-permute-start | bytes 3145736 | tf_op jit(solution)/shard_map/ppermute | solution.py:149
  20.6 53.7 %collective-permute-start.4 = (bf16[512,1024]{1,0:T(8,128)(2,1)S(1)}, bf16[512,1024]{1,0:T(8,128)(2,1)}, u32[]{:S(2)}, u32[]{:S(2)}) collective-permute-start(bf16[512,1024]{1,0:T(8,128)(2,1)S(1)} %get-tuple-element.11), channel_id=1, source_target_pairs={{0,4},{4,8},{8,12},{12,14},{14,10},{10,6},{6,2},{2,0},{1,5},{5,9},... | collective-permute-start | bytes 3145736 | tf_op jit(solution)/shard_map/ppermute | solution.py:149
  61.3 26.3 %collective-permute-start.14 = (bf16[512,1024]{1,0:T(8,128)(2,1)}, bf16[512,1024]{1,0:T(8,128)(2,1)S(1)}, u32[]{:S(2)}, u32[]{:S(2)}) collective-permute-start(bf16[512,1024]{1,0:T(8,128)(2,1)} %collective-permute-done.12), channel_id=1, source_target_pairs={{4,0},{8,4},{12,8},{14,12},{10,14},{6,10},{2,6},{0,2},{5,1},{9,5},... | collective-permute-start | bytes 3145736 | tf_op jit(solution)/shard_map/ppermute | solution.py:149
  62.9 26.2 %collective-permute-start.13 = (bf16[512,1024]{1,0:T(8,128)(2,1)}, bf16[512,1024]{1,0:T(8,128)(2,1)S(1)}, u32[]{:S(2)}, u32[]{:S(2)}) collective-permute-start(bf16[512,1024]{1,0:T(8,128)(2,1)} %collective-permute-done.11), channel_id=1, source_target_pairs={{0,4},{4,8},{8,12},{12,14},{14,10},{10,6},{6,2},{2,0},{1,5},{5,9},... | collective-permute-start | bytes 3145736 | tf_op jit(solution)/shard_map/ppermute | solution.py:149
  63.4 46.7 %collective-permute-start.7 = (bf16[512,1024]{1,0:T(8,128)(2,1)}, bf16[512,1024]{1,0:T(8,128)(2,1)S(1)}, u32[]{:S(2)}, u32[]{:S(2)}) collective-permute-start(bf16[512,1024]{1,0:T(8,128)(2,1)} %collective-permute-done.5), channel_id=1, source_target_pairs={{4,0},{8,4},{12,8},{14,12},{10,14},{6,10},{2,6},{0,2},{5,1},{9,5},... | collective-permute-start | bytes 3145736 | tf_op jit(solution)/shard_map/ppermute | solution.py:149
  74.3 40.4 %collective-permute-start.6 = (bf16[512,1024]{1,0:T(8,128)(2,1)}, bf16[512,1024]{1,0:T(8,128)(2,1)S(1)}, u32[]{:S(2)}, u32[]{:S(2)}) collective-permute-start(bf16[512,1024]{1,0:T(8,128)(2,1)} %collective-permute-done.4), channel_id=1, source_target_pairs={{0,4},{4,8},{8,12},{12,14},{14,10},{10,6},{6,2},{2,0},{1,5},{5,9},... | collective-permute-start | bytes 3145736 | tf_op jit(solution)/shard_map/ppermute | solution.py:149
  87.6 47.1 %collective-permute-start.16 = (bf16[512,1024]{1,0:T(8,128)(2,1)S(1)}, bf16[512,1024]{1,0:T(8,128)(2,1)S(1)}, u32[]{:S(2)}, u32[]{:S(2)}) collective-permute-start(bf16[512,1024]{1,0:T(8,128)(2,1)S(1)} %collective-permute-done.14), channel_id=1, source_target_pairs={{4,0},{8,4},{12,8},{14,12},{10,14},{6,10},{2,6},{0,2},{5,1},{9,5},... | collective-permute-start | bytes 3145736 | tf_op jit(solution)/shard_map/ppermute | solution.py:149
  89.1 45.0 %collective-permute-start.15 = (bf16[512,1024]{1,0:T(8,128)(2,1)S(1)}, bf16[512,1024]{1,0:T(8,128)(2,1)}, u32[]{:S(2)}, u32[]{:S(2)}) collective-permute-start(bf16[512,1024]{1,0:T(8,128)(2,1)S(1)} %collective-permute-done.13), channel_id=1, source_target_pairs={{0,4},{4,8},{8,12},{12,14},{14,10},{10,6},{6,2},{2,0},{1,5},{5,9},... | collective-permute-start | bytes 3145736 | tf_op jit(solution)/shard_map/ppermute | solution.py:149
  110.0 44.3 %collective-permute-start.9 = (bf16[512,1024]{1,0:T(8,128)(2,1)S(1)}, bf16[512,1024]{1,0:T(8,128)(2,1)}, u32[]{:S(2)}, u32[]{:S(2)}) collective-permute-start(bf16[512,1024]{1,0:T(8,128)(2,1)S(1)} %collective-permute-done.7), channel_id=1, source_target_pairs={{4,0},{8,4},{12,8},{14,12},{10,14},{6,10},{2,6},{0,2},{5,1},{9,5},... | collective-permute-start | bytes 3145736 | tf_op jit(solution)/shard_map/ppermute | solution.py:149
  114.7 52.8 %collective-permute-start.8 = (bf16[512,1024]{1,0:T(8,128)(2,1)S(1)}, bf16[512,1024]{1,0:T(8,128)(2,1)}, u32[]{:S(2)}, u32[]{:S(2)}) collective-permute-start(bf16[512,1024]{1,0:T(8,128)(2,1)S(1)} %collective-permute-done.6), channel_id=1, source_target_pairs={{0,4},{4,8},{8,12},{12,14},{14,10},{10,6},{6,2},{2,0},{1,5},{5,9},... | collective-permute-start | bytes 3145736 | tf_op jit(solution)/shard_map/ppermute | solution.py:149
  134.2 43.9 %collective-permute-start.17 = (bf16[512,1024]{1,0:T(8,128)(2,1)}, bf16[512,1024]{1,0:T(8,128)(2,1)}, u32[]{:S(2)}, u32[]{:S(2)}) collective-permute-start(bf16[512,1024]{1,0:T(8,128)(2,1)} %collective-permute-done.15), channel_id=1, source_target_pairs={{0,4},{4,8},{8,12},{12,14},{14,10},{10,6},{6,2},{2,0},{1,5},{5,9},... | collective-permute-start | bytes 3145736 | tf_op jit(solution)/shard_map/ppermute | solution.py:149
  154.3 31.9 %collective-permute-start.10 = (bf16[512,1024]{1,0:T(8,128)(2,1)}, bf16[512,1024]{1,0:T(8,128)(2,1)S(1)}, u32[]{:S(2)}, u32[]{:S(2)}) collective-permute-start(bf16[512,1024]{1,0:T(8,128)(2,1)} %collective-permute-done.9), channel_id=1, source_target_pairs={{4,0},{8,4},{12,8},{14,12},{10,14},{6,10},{2,6},{0,2},{5,1},{9,5},... | collective-permute-start | bytes 3145736 | tf_op jit(solution)/shard_map/ppermute | solution.py:149
  191.4 33.2 %all-to-all-start = ((bf16[8,64,1152]{2,1,0:T(8,128)(2,1)}), bf16[8,64,1152]{2,1,0:T(8,128)(2,1)S(1)}, u32[]{:S(2)}, u32[]{:S(2)}) async-start(bf16[8,64,1152]{2,1,0:T(8,128)(2,1)} %bitcast.20), calls=%async_computation | async-start | bytes 2359296 | tf_op jit(solution)/shard_map/all_to_all | solution.py:164
  236.9 18.3 %all-to-all-start.1 = ((bf16[32,8,1024]{2,0,1:T(8,128)(2,1)}), bf16[32,8,1024]{2,0,1:T(8,128)(2,1)S(1)}, u32[]{:S(2)}, u32[]{:S(2)}) async-start(bf16[32,8,1024]{2,0,1:T(8,128)(2,1)} %copy.73), calls=%async_computation.1 | async-start | bytes 1048576 | tf_op jit(solution)/shard_map/all_to_all | solution.py:183
  255.2 18.5 %all-to-all-start.2 = ((bf16[32,8,1024]{2,0,1:T(8,128)(2,1)}), bf16[32,8,1024]{2,0,1:T(8,128)(2,1)S(1)}, u32[]{:S(2)}, u32[]{:S(2)}) async-start(bf16[32,8,1024]{2,0,1:T(8,128)(2,1)} %copy.76), calls=%async_computation.2 | async-start | bytes 1048576 | tf_op jit(solution)/shard_map/all_to_all | solution.py:183
  277.6 25.9 %collective-permute-start.20 = (bf16[512,1024]{1,0:T(8,128)(2,1)}, bf16[512,1024]{1,0:T(8,128)(2,1)}, u32[]{:S(2)}, u32[]{:S(2)}) collective-permute-start(bf16[512,1024]{1,0:T(8,128)(2,1)} %fusion.95), channel_id=1, source_target_pairs={{0,4},{4,8},{8,12},{12,14},{14,10},{10,6},{6,2},{2,0},{1,5},{5,9},... | collective-permute-start | bytes 3145736 | tf_op jit(solution)/shard_map/ppermute | solution.py:199
  283.4 29.2 %collective-permute-start.31 = (bf16[512,1024]{1,0:T(8,128)(2,1)S(1)}, bf16[512,1024]{1,0:T(8,128)(2,1)}, u32[]{:S(2)}, u32[]{:S(2)}) collective-permute-start(bf16[512,1024]{1,0:T(8,128)(2,1)S(1)} %fusion.101), channel_id=1, source_target_pairs={{4,0},{8,4},{12,8},{14,12},{10,14},{6,10},{2,6},{0,2},{5,1},{9,5},... | collective-permute-start | bytes 3145736 | tf_op jit(solution)/shard_map/ppermute | solution.py:199
  292.1 39.9 %collective-permute-start.24 = (bf16[512,1024]{1,0:T(8,128)(2,1)}, bf16[512,1024]{1,0:T(8,128)(2,1)}, u32[]{:S(2)}, u32[]{:S(2)}) collective-permute-start(bf16[512,1024]{1,0:T(8,128)(2,1)} %fusion.98), channel_id=1, source_target_pairs={{4,0},{8,4},{12,8},{14,12},{10,14},{6,10},{2,6},{0,2},{5,1},{9,5},... | collective-permute-start | bytes 3145736 | tf_op jit(solution)/shard_map/ppermute | solution.py:199
  307.5 29.9 %collective-permute-start.21 = (bf16[512,1024]{1,0:T(8,128)(2,1)}, bf16[512,1024]{1,0:T(8,128)(2,1)}, u32[]{:S(2)}, u32[]{:S(2)}) collective-permute-start(bf16[512,1024]{1,0:T(8,128)(2,1)} %add_convert_fusion.10), channel_id=1, source_target_pairs={{0,4},{4,8},{8,12},{12,14},{14,10},{10,6},{6,2},{2,0},{1,5},{5,9},... | collective-permute-start | bytes 3145736 | tf_op jit(solution)/shard_map/ppermute | solution.py:199
  312.3 44.1 %collective-permute-start.28 = (bf16[512,1024]{1,0:T(8,128)(2,1)}, bf16[512,1024]{1,0:T(8,128)(2,1)}, u32[]{:S(2)}, u32[]{:S(2)}) collective-permute-start(bf16[512,1024]{1,0:T(8,128)(2,1)} %fusion.92), channel_id=1, source_target_pairs={{0,4},{4,8},{8,12},{12,14},{14,10},{10,6},{6,2},{2,0},{1,5},{5,9},... | collective-permute-start | bytes 3145736 | tf_op jit(solution)/shard_map/ppermute | solution.py:199
  315.9 45.5 %collective-permute-start.32 = (bf16[512,1024]{1,0:T(8,128)(2,1)S(1)}, bf16[512,1024]{1,0:T(8,128)(2,1)}, u32[]{:S(2)}, u32[]{:S(2)}) collective-permute-start(bf16[512,1024]{1,0:T(8,128)(2,1)S(1)} %add_convert_fusion.3), channel_id=1, source_target_pairs={{4,0},{8,4},{12,8},{14,12},{10,14},{6,10},{2,6},{0,2},{5,1},{9,5},... | collective-permute-start | bytes 3145736 | tf_op jit(solution)/shard_map/ppermute | solution.py:199
  336.1 40.9 %collective-permute-start.25 = (bf16[512,1024]{1,0:T(8,128)(2,1)}, bf16[512,1024]{1,0:T(8,128)(2,1)}, u32[]{:S(2)}, u32[]{:S(2)}) collective-permute-start(bf16[512,1024]{1,0:T(8,128)(2,1)} %add_convert_fusion.7), channel_id=1, source_target_pairs={{4,0},{8,4},{12,8},{14,12},{10,14},{6,10},{2,6},{0,2},{5,1},{9,5},... | collective-permute-start | bytes 3145736 | tf_op jit(solution)/shard_map/ppermute | solution.py:199
  341.5 41.1 %collective-permute-start.22 = (bf16[512,1024]{1,0:T(8,128)(2,1)}, bf16[512,1024]{1,0:T(8,128)(2,1)}, u32[]{:S(2)}, u32[]{:S(2)}) collective-permute-start(bf16[512,1024]{1,0:T(8,128)(2,1)} %add_convert_fusion.9), channel_id=1, source_target_pairs={{0,4},{4,8},{8,12},{12,14},{14,10},{10,6},{6,2},{2,0},{1,5},{5,9},... | collective-permute-start | bytes 3145736 | tf_op jit(solution)/shard_map/ppermute | solution.py:199
  360.6 40.7 %collective-permute-start.29 = (bf16[512,1024]{1,0:T(8,128)(2,1)}, bf16[512,1024]{1,0:T(8,128)(2,1)}, u32[]{:S(2)}, u32[]{:S(2)}) collective-permute-start(bf16[512,1024]{1,0:T(8,128)(2,1)} %add_convert_fusion.5), channel_id=1, source_target_pairs={{0,4},{4,8},{8,12},{12,14},{14,10},{10,6},{6,2},{2,0},{1,5},{5,9},... | collective-permute-start | bytes 3145736 | tf_op jit(solution)/shard_map/ppermute | solution.py:199
  365.7 40.7 %collective-permute-start.33 = (bf16[512,1024]{1,0:T(8,128)(2,1)}, bf16[512,1024]{1,0:T(8,128)(2,1)}, u32[]{:S(2)}, u32[]{:S(2)}) collective-permute-start(bf16[512,1024]{1,0:T(8,128)(2,1)} %add_convert_fusion.2), channel_id=1, source_target_pairs={{4,0},{8,4},{12,8},{14,12},{10,14},{6,10},{2,6},{0,2},{5,1},{9,5},... | collective-permute-start | bytes 3145736 | tf_op jit(solution)/shard_map/ppermute | solution.py:199
  381.1 40.8 %collective-permute-start.26 = (bf16[512,1024]{1,0:T(8,128)(2,1)}, bf16[512,1024]{1,0:T(8,128)(2,1)S(1)}, u32[]{:S(2)}, u32[]{:S(2)}) collective-permute-start(bf16[512,1024]{1,0:T(8,128)(2,1)} %add_convert_fusion.6), channel_id=1, source_target_pairs={{4,0},{8,4},{12,8},{14,12},{10,14},{6,10},{2,6},{0,2},{5,1},{9,5},... | collective-permute-start | bytes 3145736 | tf_op jit(solution)/shard_map/ppermute | solution.py:199
  386.7 37.1 %collective-permute-start.23 = (bf16[512,1024]{1,0:T(8,128)(2,1)}, bf16[512,1024]{1,0:T(8,128)(2,1)}, u32[]{:S(2)}, u32[]{:S(2)}) collective-permute-start(bf16[512,1024]{1,0:T(8,128)(2,1)} %add_convert_fusion.8), channel_id=1, source_target_pairs={{0,4},{4,8},{8,12},{12,14},{14,10},{10,6},{6,2},{2,0},{1,5},{5,9},... | collective-permute-start | bytes 3145736 | tf_op jit(solution)/shard_map/ppermute | solution.py:199
  405.6 39.4 %collective-permute-start.30 = (bf16[512,1024]{1,0:T(8,128)(2,1)}, bf16[512,1024]{1,0:T(8,128)(2,1)}, u32[]{:S(2)}, u32[]{:S(2)}) collective-permute-start(bf16[512,1024]{1,0:T(8,128)(2,1)} %add_convert_fusion.4), channel_id=1, source_target_pairs={{0,4},{4,8},{8,12},{12,14},{14,10},{10,6},{6,2},{2,0},{1,5},{5,9},... | collective-permute-start | bytes 3145736 | tf_op jit(solution)/shard_map/ppermute | solution.py:199
  410.6 34.4 %collective-permute-start.34 = (bf16[512,1024]{1,0:T(8,128)(2,1)}, bf16[512,1024]{1,0:T(8,128)(2,1)}, u32[]{:S(2)}, u32[]{:S(2)}) collective-permute-start(bf16[512,1024]{1,0:T(8,128)(2,1)} %add_convert_fusion.1), channel_id=1, source_target_pairs={{4,0},{8,4},{12,8},{14,12},{10,14},{6,10},{2,6},{0,2},{5,1},{9,5},... | collective-permute-start | bytes 3145736 | tf_op jit(solution)/shard_map/ppermute | solution.py:199
  (20 other events, 227.2 us)

commit v5 on v4

--- a/solution.py
+++ b/solution.py
@@ -170,6 +170,12 @@
     key_span_width = keyvals.shape[1] // 2
     part_rows = rows_here // 2
     head_rows = []
+    ready = {}
+
+    def term(half, dest):
+        block = lax.dynamic_index_in_dim(out_blocks, at_place(dest), 0, keepdims=False)
+        return jnp.dot(head_rows[half], block, preferred_element_type=jnp.float32)
+
     for part in (0, 1):
         span = slice(part * part_rows, (part + 1) * part_rows)
         attended = attend(
@@ -180,20 +186,23 @@
             cached_value_rows[span],
             lengths[span],
         )
+        if part == 1:
+            for chain in chains[:2]:
+                first = term(0, chain[0] * reach[chain]).astype(jnp.bfloat16)
+                ready[chain], attended = lax.optimization_barrier((first, attended))
         own_rows = lax.all_to_all(attended, "gx", split_axis=1, concat_axis=0, tiled=True)
         other_rows = lax.ppermute(own_rows, "gy", pair)
         head_rows.append(jnp.concatenate([own_rows, other_rows], axis=0))
     parted = states.reshape(2, size, 2, part_rows, width)
 
-    def term(half, dest):
-        block = lax.dynamic_index_in_dim(out_blocks, at_place(dest), 0, keepdims=False)
-        return jnp.dot(head_rows[half], block, preferred_element_type=jnp.float32)
-
     moving = {}
     for step in range(long_way, 0, -1):
         for chain in chains:
             if step <= reach[chain]:
-                value = term(chain[1], chain[0] * step)
+                if chain in ready:
+                    value = ready.pop(chain)
+                else:
+                    value = term(chain[1], chain[0] * step)
                 if chain in moving:
                     value = value + moving[chain].astype(jnp.float32)
                 moving[chain] = lax.ppermute(value.astype(jnp.bfloat16), "gx", hops[chain[0]])

time: 459 us -> 466 us (1.015)
  blocking collectives: 0 us -> 18.6 us
  waiting for transfers between devices: 196 us -> 188 us
    all_to_all x0 -> x1, blocking collectives: none -> 18.6 us  [shards(): lax.all_to_all(attended, 'gx', split_axis=1, concat_axis=0, tiled=True)]
    all_to_all x2 -> x1, waiting for transfers between devices: 19 us -> 10.4 us  [shards(): lax.all_to_all(attended, 'gx', split_axis=1, concat_axis=0, tiled=True)]
    unnamed x29 -> x34, local copies, waits for them, and re-layouts: 19.8 us -> 20.2 us
  transfers between devices with their start and end apart: 38 -> 37, of which waited for: 19 -> 18; matrix products, arithmetic and copies ran while one was open for 35% -> 33% of each run, Pallas kernels for 0% -> 0%
where the time goes in v5:
time: 466 us; the launch traced here: 457 us
  waiting for transfers between devices  188 us (40%)
  matrix products  134 us (29%)
  starting transfers between devices  45.9 us (10%)
  local copies, waits for them, and re-layouts  30.9 us (7%)
  between operations  27.4 us (6%)
  blocking collectives  18.6 us (4%)
  other arithmetic  11.9 us (3%)
    ppermute x14, waiting for transfers between devices, shards(): lax.ppermute(value.astype(jnp.bfloat16), 'gx', hops[chain[0]])  83 us
    ppermute x14, waiting for transfers between devices, shards(): arrived[chain] = lax.ppermute(held[chain], 'gx', hops[chain[0]])  64.3 us
    dot_general x16, matrix products, term(): return jnp.dot(head_rows[half], block, preferred_element_type=jnp.float32)  61.6 us
    dot_general x16, matrix products, project(): jnp.dot(normed, wq, preferred_element_type=jnp.float32)  40.5 us
    all_to_all x1, waiting for transfers between devices, shards(): lax.all_to_all(mine.reshape(size, rows_here, mine.shape[1]), 'gx', split_...  25.5 us
    dot_general x16, matrix products, project(): jnp.dot(normed, wkv, preferred_element_type=jnp.float32)  21.5 us
    unnamed x34, local copies, waits for them, and re-layouts  20.2 us
    all_to_all x1, blocking collectives, shards(): lax.all_to_all(attended, 'gx', split_axis=1, concat_axis=0, tiled=True)  18.6 us
  transfers between devices with their start and end apart: 37, of which 18 were waited for; matrix products, arithmetic and copies ran while one was open for 33% of the time, Pallas kernels for 0%

profile of v5, /device:TPU:0, one launch (start us, length us, event | category | flops | bytes accessed | tf_op | source)
XLA Modules:
  0.0 456.9 jit_solution(16461482512585221503)
XLA Ops:
  32.3 18.7 %copy.133 = bf16[1024,1,8,1024]{3,0,2,1:T(8,128)(2,1)} copy(bf16[1024,1,8,1024]{3,2,1,0:T(8,128)(2,1)} %param.14) | data formatting | bytes 33554432 | tf_op args[4]
  83.5 3.9 collective-permute-done.14
  89.5 20.4 %collective-permute-done.7 = bf16[512,1024]{1,0:T(8,128)(2,1)S(1)} collective-permute-done((bf16[512,1024]{1,0:T(8,128)(2,1)}, bf16[512,1024]{1,0:T(8,128)(2,1)S(1)}, u32[]{:S(2)}, u32[]{:S(2)}) %collective-permute-start.7) | collective-permute-done | bytes 1048608 | tf_op jit(solution)/shard_map/ppermute | solution.py:149
  120.0 14.0 %collective-permute-done.15 = bf16[512,1024]{1,0:T(8,128)(2,1)} collective-permute-done((bf16[512,1024]{1,0:T(8,128)(2,1)S(1)}, bf16[512,1024]{1,0:T(8,128)(2,1)}, u32[]{:S(2)}, u32[]{:S(2)}) %collective-permute-start.15) | collective-permute-done | bytes 1048608 | tf_op jit(solution)/shard_map/ppermute | solution.py:149
  136.4 17.8 %collective-permute-done.9 = bf16[512,1024]{1,0:T(8,128)(2,1)} collective-permute-done((bf16[512,1024]{1,0:T(8,128)(2,1)S(1)}, bf16[512,1024]{1,0:T(8,128)(2,1)}, u32[]{:S(2)}, u32[]{:S(2)}) %collective-permute-start.9) | collective-permute-done | bytes 1048608 | tf_op jit(solution)/shard_map/ppermute | solution.py:149
  160.8 3.8 fusion.68
  169.7 8.2 %collective-permute-done.17 = bf16[512,1024]{1,0:T(8,128)(2,1)} collective-permute-done((bf16[512,1024]{1,0:T(8,128)(2,1)}, bf16[512,1024]{1,0:T(8,128)(2,1)}, u32[]{:S(2)}, u32[]{:S(2)}) %collective-permute-start.17) | collective-permute-done | bytes 1048608 | tf_op jit(solution)/shard_map/ppermute | solution.py:149
  177.9 4.4 add_convert_fusion.11
  191.2 4.0 all-to-all-start
  199.1 25.5 %all-to-all-done = bf16[8,64,1152]{2,1,0:T(8,128)(2,1)S(1)} async-done(((bf16[8,64,1152]{2,1,0:T(8,128)(2,1)}), bf16[8,64,1152]{2,1,0:T(8,128)(2,1)S(1)}, u32[]{:S(2)}, u32[]{:S(2)}) %all-to-all-start) | async-done | bytes 1179680 | tf_op jit(solution)/shard_map/all_to_all | solution.py:164
  237.0 3.8 all-to-all-start.1
  245.1 10.4 %all-to-all-done.1 = bf16[32,8,1024]{2,0,1:T(8,128)(2,1)S(1)} async-done(((bf16[32,8,1024]{2,0,1:T(8,128)(2,1)}), bf16[32,8,1024]{2,0,1:T(8,128)(2,1)S(1)}, u32[]{:S(2)}, u32[]{:S(2)}) %all-to-all-start.1) | async-done | bytes 524320 | tf_op jit(solution)/shard_map/all_to_all | solution.py:193
  258.4 4.0 fusion.95
  265.5 18.6 %all_to_all.43 = bf16[32,8,1024]{2,0,1:T(8,128)(2,1)S(1)} all-to-all(bf16[32,8,1024]{2,0,1:T(8,128)(2,1)S(1)} %bitcast.180), channel_id=1, replica_groups=mesh['groups'=2,'gx'=8,'gy'=2] {'gx'}, dimensions={1} | all-to-all | bytes 1048576 | tf_op jit(solution)/shard_map/all_to_all | solution.py:193
  287.1 4.0 fusion.101
  295.3 14.7 %collective-permute-done.20 = bf16[512,1024]{1,0:T(8,128)(2,1)} collective-permute-done((bf16[512,1024]{1,0:T(8,128)(2,1)}, bf16[512,1024]{1,0:T(8,128)(2,1)}, u32[]{:S(2)}, u32[]{:S(2)}) %collective-permute-start.20) | collective-permute-done | bytes 1048608 | tf_op jit(solution)/shard_map/ppermute | solution.py:208
  310.0 4.1 add_convert_fusion.10
  315.2 4.0 fusion.92
  319.5 4.2 add_convert_fusion.3
  329.3 10.6 %collective-permute-done.24 = bf16[512,1024]{1,0:T(8,128)(2,1)} collective-permute-done((bf16[512,1024]{1,0:T(8,128)(2,1)S(1)}, bf16[512,1024]{1,0:T(8,128)(2,1)}, u32[]{:S(2)}, u32[]{:S(2)}) %collective-permute-start.24) | collective-permute-done | bytes 1048608 | tf_op jit(solution)/shard_map/ppermute | solution.py:208
  344.2 4.1 add_convert_fusion.9
  349.4 13.5 %collective-permute-done.28 = bf16[512,1024]{1,0:T(8,128)(2,1)} collective-permute-done((bf16[512,1024]{1,0:T(8,128)(2,1)}, bf16[512,1024]{1,0:T(8,128)(2,1)}, u32[]{:S(2)}, u32[]{:S(2)}) %collective-permute-start.28) | collective-permute-done | bytes 1048608 | tf_op jit(solution)/shard_map/ppermute | solution.py:208
  362.9 4.2 add_convert_fusion.5
  368.3 4.2 add_convert_fusion.2
  377.2 7.7 %collective-permute-done.25 = bf16[512,1024]{1,0:T(8,128)(2,1)} collective-permute-done((bf16[512,1024]{1,0:T(8,128)(2,1)S(1)}, bf16[512,1024]{1,0:T(8,128)(2,1)}, u32[]{:S(2)}, u32[]{:S(2)}) %collective-permute-start.25) | collective-permute-done | bytes 1048608 | tf_op jit(solution)/shard_map/ppermute | solution.py:208
  384.8 4.1 add_convert_fusion.6
  389.8 4.1 add_convert_fusion.8
  395.1 12.8 %collective-permute-done.29 = bf16[512,1024]{1,0:T(8,128)(2,1)} collective-permute-done((bf16[512,1024]{1,0:T(8,128)(2,1)}, bf16[512,1024]{1,0:T(8,128)(2,1)}, u32[]{:S(2)}, u32[]{:S(2)}) %collective-permute-start.29) | collective-permute-done | bytes 1048608 | tf_op jit(solution)/shard_map/ppermute | solution.py:208
  407.9 4.2 add_convert_fusion.4
  413.2 4.2 add_convert_fusion.1
  426.1 3.5 collective-permute-done.26
  432.1 19.4 %collective-permute-done.30 = bf16[512,1024]{1,0:T(8,128)(2,1)} collective-permute-done((bf16[512,1024]{1,0:T(8,128)(2,1)}, bf16[512,1024]{1,0:T(8,128)(2,1)}, u32[]{:S(2)}, u32[]{:S(2)}) %collective-permute-start.30) | collective-permute-done | bytes 1048608 | tf_op jit(solution)/shard_map/ppermute | solution.py:208
  (185 shorter events, 144.1 us)
Async XLA Ops:
  11.3 39.7 %collective-permute-start.2 = (f32[9216]{0:T(1024)S(1)}, f32[9216]{0:T(1024)S(1)}, u32[]{:S(2)}, u32[]{:S(2)}) collective-permute-start(f32[9216]{0:T(1024)S(1)} %add.460), channel_id=1, source_target_pairs={{0,8},{2,10},{4,12},{6,14},{8,0},{10,2},{12,4},{14,6},{1,9},{3,11}... | collective-permute-start | bytes 110600 | tf_op jit(solution)/shard_map/ppermute | solution.py:112
  17.1 44.1 %collective-permute-start.12 = (bf16[512,1024]{1,0:T(8,128)(2,1)}, bf16[512,1024]{1,0:T(8,128)(2,1)}, u32[]{:S(2)}, u32[]{:S(2)}) collective-permute-start(bf16[512,1024]{1,0:T(8,128)(2,1)} %get-tuple-element.20), channel_id=1, source_target_pairs={{4,0},{8,4},{12,8},{14,12},{10,14},{6,10},{2,6},{0,2},{5,1},{9,5},... | collective-permute-start | bytes 3145736 | tf_op jit(solution)/shard_map/ppermute | solution.py:149
  18.6 44.1 %collective-permute-start.11 = (bf16[512,1024]{1,0:T(8,128)(2,1)}, bf16[512,1024]{1,0:T(8,128)(2,1)}, u32[]{:S(2)}, u32[]{:S(2)}) collective-permute-start(bf16[512,1024]{1,0:T(8,128)(2,1)} %get-tuple-element.20), channel_id=1, source_target_pairs={{0,4},{4,8},{8,12},{12,14},{14,10},{10,6},{6,2},{2,0},{1,5},{5,9},... | collective-permute-start | bytes 3145736 | tf_op jit(solution)/shard_map/ppermute | solution.py:149
  19.1 44.1 %collective-permute-start.5 = (bf16[512,1024]{1,0:T(8,128)(2,1)S(1)}, bf16[512,1024]{1,0:T(8,128)(2,1)}, u32[]{:S(2)}, u32[]{:S(2)}) collective-permute-start(bf16[512,1024]{1,0:T(8,128)(2,1)S(1)} %get-tuple-element.19), channel_id=1, source_target_pairs={{4,0},{8,4},{12,8},{14,12},{10,14},{6,10},{2,6},{0,2},{5,1},{9,5},... | collective-permute-start | bytes 3145736 | tf_op jit(solution)/shard_map/ppermute | solution.py:149
  20.6 53.6 %collective-permute-start.4 = (bf16[512,1024]{1,0:T(8,128)(2,1)S(1)}, bf16[512,1024]{1,0:T(8,128)(2,1)}, u32[]{:S(2)}, u32[]{:S(2)}) collective-permute-start(bf16[512,1024]{1,0:T(8,128)(2,1)S(1)} %get-tuple-element.19), channel_id=1, source_target_pairs={{0,4},{4,8},{8,12},{12,14},{14,10},{10,6},{6,2},{2,0},{1,5},{5,9},... | collective-permute-start | bytes 3145736 | tf_op jit(solution)/shard_map/ppermute | solution.py:149
  61.2 26.3 %collective-permute-start.14 = (bf16[512,1024]{1,0:T(8,128)(2,1)}, bf16[512,1024]{1,0:T(8,128)(2,1)S(1)}, u32[]{:S(2)}, u32[]{:S(2)}) collective-permute-start(bf16[512,1024]{1,0:T(8,128)(2,1)} %collective-permute-done.12), channel_id=1, source_target_pairs={{4,0},{8,4},{12,8},{14,12},{10,14},{6,10},{2,6},{0,2},{5,1},{9,5},... | collective-permute-start | bytes 3145736 | tf_op jit(solution)/shard_map/ppermute | solution.py:149
  62.7 26.3 %collective-permute-start.13 = (bf16[512,1024]{1,0:T(8,128)(2,1)}, bf16[512,1024]{1,0:T(8,128)(2,1)S(1)}, u32[]{:S(2)}, u32[]{:S(2)}) collective-permute-start(bf16[512,1024]{1,0:T(8,128)(2,1)} %collective-permute-done.11), channel_id=1, source_target_pairs={{0,4},{4,8},{8,12},{12,14},{14,10},{10,6},{6,2},{2,0},{1,5},{5,9},... | collective-permute-start | bytes 3145736 | tf_op jit(solution)/shard_map/ppermute | solution.py:149
  63.3 46.6 %collective-permute-start.7 = (bf16[512,1024]{1,0:T(8,128)(2,1)}, bf16[512,1024]{1,0:T(8,128)(2,1)S(1)}, u32[]{:S(2)}, u32[]{:S(2)}) collective-permute-start(bf16[512,1024]{1,0:T(8,128)(2,1)} %collective-permute-done.5), channel_id=1, source_target_pairs={{4,0},{8,4},{12,8},{14,12},{10,14},{6,10},{2,6},{0,2},{5,1},{9,5},... | collective-permute-start | bytes 3145736 | tf_op jit(solution)/shard_map/ppermute | solution.py:149
  74.2 40.4 %collective-permute-start.6 = (bf16[512,1024]{1,0:T(8,128)(2,1)}, bf16[512,1024]{1,0:T(8,128)(2,1)S(1)}, u32[]{:S(2)}, u32[]{:S(2)}) collective-permute-start(bf16[512,1024]{1,0:T(8,128)(2,1)} %collective-permute-done.4), channel_id=1, source_target_pairs={{0,4},{4,8},{8,12},{12,14},{14,10},{10,6},{6,2},{2,0},{1,5},{5,9},... | collective-permute-start | bytes 3145736 | tf_op jit(solution)/shard_map/ppermute | solution.py:149
  87.4 47.1 %collective-permute-start.16 = (bf16[512,1024]{1,0:T(8,128)(2,1)S(1)}, bf16[512,1024]{1,0:T(8,128)(2,1)S(1)}, u32[]{:S(2)}, u32[]{:S(2)}) collective-permute-start(bf16[512,1024]{1,0:T(8,128)(2,1)S(1)} %collective-permute-done.14), channel_id=1, source_target_pairs={{4,0},{8,4},{12,8},{14,12},{10,14},{6,10},{2,6},{0,2},{5,1},{9,5},... | collective-permute-start | bytes 3145736 | tf_op jit(solution)/shard_map/ppermute | solution.py:149
  89.0 45.0 %collective-permute-start.15 = (bf16[512,1024]{1,0:T(8,128)(2,1)S(1)}, bf16[512,1024]{1,0:T(8,128)(2,1)}, u32[]{:S(2)}, u32[]{:S(2)}) collective-permute-start(bf16[512,1024]{1,0:T(8,128)(2,1)S(1)} %collective-permute-done.13), channel_id=1, source_target_pairs={{0,4},{4,8},{8,12},{12,14},{14,10},{10,6},{6,2},{2,0},{1,5},{5,9},... | collective-permute-start | bytes 3145736 | tf_op jit(solution)/shard_map/ppermute | solution.py:149
  109.9 44.3 %collective-permute-start.9 = (bf16[512,1024]{1,0:T(8,128)(2,1)S(1)}, bf16[512,1024]{1,0:T(8,128)(2,1)}, u32[]{:S(2)}, u32[]{:S(2)}) collective-permute-start(bf16[512,1024]{1,0:T(8,128)(2,1)S(1)} %collective-permute-done.7), channel_id=1, source_target_pairs={{4,0},{8,4},{12,8},{14,12},{10,14},{6,10},{2,6},{0,2},{5,1},{9,5},... | collective-permute-start | bytes 3145736 | tf_op jit(solution)/shard_map/ppermute | solution.py:149
  114.6 52.6 %collective-permute-start.8 = (bf16[512,1024]{1,0:T(8,128)(2,1)S(1)}, bf16[512,1024]{1,0:T(8,128)(2,1)}, u32[]{:S(2)}, u32[]{:S(2)}) collective-permute-start(bf16[512,1024]{1,0:T(8,128)(2,1)S(1)} %collective-permute-done.6), channel_id=1, source_target_pairs={{0,4},{4,8},{8,12},{12,14},{14,10},{10,6},{6,2},{2,0},{1,5},{5,9},... | collective-permute-start | bytes 3145736 | tf_op jit(solution)/shard_map/ppermute | solution.py:149
  134.0 43.9 %collective-permute-start.17 = (bf16[512,1024]{1,0:T(8,128)(2,1)}, bf16[512,1024]{1,0:T(8,128)(2,1)}, u32[]{:S(2)}, u32[]{:S(2)}) collective-permute-start(bf16[512,1024]{1,0:T(8,128)(2,1)} %collective-permute-done.15), channel_id=1, source_target_pairs={{0,4},{4,8},{8,12},{12,14},{14,10},{10,6},{6,2},{2,0},{1,5},{5,9},... | collective-permute-start | bytes 3145736 | tf_op jit(solution)/shard_map/ppermute | solution.py:149
  154.2 31.8 %collective-permute-start.10 = (bf16[512,1024]{1,0:T(8,128)(2,1)}, bf16[512,1024]{1,0:T(8,128)(2,1)S(1)}, u32[]{:S(2)}, u32[]{:S(2)}) collective-permute-start(bf16[512,1024]{1,0:T(8,128)(2,1)} %collective-permute-done.9), channel_id=1, source_target_pairs={{4,0},{8,4},{12,8},{14,12},{10,14},{6,10},{2,6},{0,2},{5,1},{9,5},... | collective-permute-start | bytes 3145736 | tf_op jit(solution)/shard_map/ppermute | solution.py:149
  184.2 5.7 %collective-permute-start.18 = (bf16[512,1152]{1,0:T(8,128)(2,1)S(1)}, bf16[512,1152]{1,0:T(8,128)(2,1)S(1)}, u32[]{:S(2)}, u32[]{:S(2)}) collective-permute-start(bf16[512,1152]{1,0:T(8,128)(2,1)S(1)} %pad_maximum_fusion.1), channel_id=1, source_target_pairs={{0,1},{1,0},{2,3},{3,2},{4,5},{5,4},{6,7},{7,6},{8,9},{9,8},{10,11... | collective-permute-start | bytes 3538952 | tf_op jit(solution)/shard_map/ppermute | solution.py:159
  191.2 33.4 %all-to-all-start = ((bf16[8,64,1152]{2,1,0:T(8,128)(2,1)}), bf16[8,64,1152]{2,1,0:T(8,128)(2,1)S(1)}, u32[]{:S(2)}, u32[]{:S(2)}) async-start(bf16[8,64,1152]{2,1,0:T(8,128)(2,1)} %bitcast.20), calls=%async_computation | async-start | bytes 2359296 | tf_op jit(solution)/shard_map/all_to_all | solution.py:164
  237.0 18.5 %all-to-all-start.1 = ((bf16[32,8,1024]{2,0,1:T(8,128)(2,1)}), bf16[32,8,1024]{2,0,1:T(8,128)(2,1)S(1)}, u32[]{:S(2)}, u32[]{:S(2)}) async-start(bf16[32,8,1024]{2,0,1:T(8,128)(2,1)} %copy.95), calls=%async_computation.1 | async-start | bytes 1048576 | tf_op jit(solution)/shard_map/all_to_all | solution.py:193
  284.1 25.9 %collective-permute-start.20 = (bf16[512,1024]{1,0:T(8,128)(2,1)}, bf16[512,1024]{1,0:T(8,128)(2,1)}, u32[]{:S(2)}, u32[]{:S(2)}) collective-permute-start(bf16[512,1024]{1,0:T(8,128)(2,1)} %fusion.95), channel_id=1, source_target_pairs={{0,4},{4,8},{8,12},{12,14},{14,10},{10,6},{6,2},{2,0},{1,5},{5,9},... | collective-permute-start | bytes 3145736 | tf_op jit(solution)/shard_map/ppermute | solution.py:208
  291.1 28.4 %collective-permute-start.31 = (bf16[512,1024]{1,0:T(8,128)(2,1)}, bf16[512,1024]{1,0:T(8,128)(2,1)}, u32[]{:S(2)}, u32[]{:S(2)}) collective-permute-start(bf16[512,1024]{1,0:T(8,128)(2,1)} %fusion.101), channel_id=1, source_target_pairs={{4,0},{8,4},{12,8},{14,12},{10,14},{6,10},{2,6},{0,2},{5,1},{9,5},... | collective-permute-start | bytes 3145736 | tf_op jit(solution)/shard_map/ppermute | solution.py:208
  293.7 46.2 %collective-permute-start.24 = (bf16[512,1024]{1,0:T(8,128)(2,1)S(1)}, bf16[512,1024]{1,0:T(8,128)(2,1)}, u32[]{:S(2)}, u32[]{:S(2)}) collective-permute-start(bf16[512,1024]{1,0:T(8,128)(2,1)S(1)} %fusion.98), channel_id=1, source_target_pairs={{4,0},{8,4},{12,8},{14,12},{10,14},{6,10},{2,6},{0,2},{5,1},{9,5},... | collective-permute-start | bytes 3145736 | tf_op jit(solution)/shard_map/ppermute | solution.py:208
  314.1 30.1 %collective-permute-start.21 = (bf16[512,1024]{1,0:T(8,128)(2,1)}, bf16[512,1024]{1,0:T(8,128)(2,1)}, u32[]{:S(2)}, u32[]{:S(2)}) collective-permute-start(bf16[512,1024]{1,0:T(8,128)(2,1)} %add_convert_fusion.10), channel_id=1, source_target_pairs={{0,4},{4,8},{8,12},{12,14},{14,10},{10,6},{6,2},{2,0},{1,5},{5,9},... | collective-permute-start | bytes 3145736 | tf_op jit(solution)/shard_map/ppermute | solution.py:208
  319.2 43.7 %collective-permute-start.28 = (bf16[512,1024]{1,0:T(8,128)(2,1)}, bf16[512,1024]{1,0:T(8,128)(2,1)}, u32[]{:S(2)}, u32[]{:S(2)}) collective-permute-start(bf16[512,1024]{1,0:T(8,128)(2,1)} %fusion.92), channel_id=1, source_target_pairs={{0,4},{4,8},{8,12},{12,14},{14,10},{10,6},{6,2},{2,0},{1,5},{5,9},... | collective-permute-start | bytes 3145736 | tf_op jit(solution)/shard_map/ppermute | solution.py:208
  323.7 44.6 %collective-permute-start.32 = (bf16[512,1024]{1,0:T(8,128)(2,1)}, bf16[512,1024]{1,0:T(8,128)(2,1)}, u32[]{:S(2)}, u32[]{:S(2)}) collective-permute-start(bf16[512,1024]{1,0:T(8,128)(2,1)} %add_convert_fusion.3), channel_id=1, source_target_pairs={{4,0},{8,4},{12,8},{14,12},{10,14},{6,10},{2,6},{0,2},{5,1},{9,5},... | collective-permute-start | bytes 3145736 | tf_op jit(solution)/shard_map/ppermute | solution.py:208
  343.0 41.8 %collective-permute-start.25 = (bf16[512,1024]{1,0:T(8,128)(2,1)S(1)}, bf16[512,1024]{1,0:T(8,128)(2,1)}, u32[]{:S(2)}, u32[]{:S(2)}) collective-permute-start(bf16[512,1024]{1,0:T(8,128)(2,1)S(1)} %add_convert_fusion.7), channel_id=1, source_target_pairs={{4,0},{8,4},{12,8},{14,12},{10,14},{6,10},{2,6},{0,2},{5,1},{9,5},... | collective-permute-start | bytes 3145736 | tf_op jit(solution)/shard_map/ppermute | solution.py:208
  348.3 41.5 %collective-permute-start.22 = (bf16[512,1024]{1,0:T(8,128)(2,1)}, bf16[512,1024]{1,0:T(8,128)(2,1)}, u32[]{:S(2)}, u32[]{:S(2)}) collective-permute-start(bf16[512,1024]{1,0:T(8,128)(2,1)} %add_convert_fusion.9), channel_id=1, source_target_pairs={{0,4},{4,8},{8,12},{12,14},{14,10},{10,6},{6,2},{2,0},{1,5},{5,9},... | collective-permute-start | bytes 3145736 | tf_op jit(solution)/shard_map/ppermute | solution.py:208
  367.2 40.7 %collective-permute-start.29 = (bf16[512,1024]{1,0:T(8,128)(2,1)}, bf16[512,1024]{1,0:T(8,128)(2,1)}, u32[]{:S(2)}, u32[]{:S(2)}) collective-permute-start(bf16[512,1024]{1,0:T(8,128)(2,1)} %add_convert_fusion.5), channel_id=1, source_target_pairs={{0,4},{4,8},{8,12},{12,14},{14,10},{10,6},{6,2},{2,0},{1,5},{5,9},... | collective-permute-start | bytes 3145736 | tf_op jit(solution)/shard_map/ppermute | solution.py:208
  372.5 40.7 %collective-permute-start.33 = (bf16[512,1024]{1,0:T(8,128)(2,1)}, bf16[512,1024]{1,0:T(8,128)(2,1)}, u32[]{:S(2)}, u32[]{:S(2)}) collective-permute-start(bf16[512,1024]{1,0:T(8,128)(2,1)} %add_convert_fusion.2), channel_id=1, source_target_pairs={{4,0},{8,4},{12,8},{14,12},{10,14},{6,10},{2,6},{0,2},{5,1},{9,5},... | collective-permute-start | bytes 3145736 | tf_op jit(solution)/shard_map/ppermute | solution.py:208
  388.9 40.8 %collective-permute-start.26 = (bf16[512,1024]{1,0:T(8,128)(2,1)}, bf16[512,1024]{1,0:T(8,128)(2,1)S(1)}, u32[]{:S(2)}, u32[]{:S(2)}) collective-permute-start(bf16[512,1024]{1,0:T(8,128)(2,1)} %add_convert_fusion.6), channel_id=1, source_target_pairs={{4,0},{8,4},{12,8},{14,12},{10,14},{6,10},{2,6},{0,2},{5,1},{9,5},... | collective-permute-start | bytes 3145736 | tf_op jit(solution)/shard_map/ppermute | solution.py:208
  394.0 36.4 %collective-permute-start.23 = (bf16[512,1024]{1,0:T(8,128)(2,1)}, bf16[512,1024]{1,0:T(8,128)(2,1)}, u32[]{:S(2)}, u32[]{:S(2)}) collective-permute-start(bf16[512,1024]{1,0:T(8,128)(2,1)} %add_convert_fusion.8), channel_id=1, source_target_pairs={{0,4},{4,8},{8,12},{12,14},{14,10},{10,6},{6,2},{2,0},{1,5},{5,9},... | collective-permute-start | bytes 3145736 | tf_op jit(solution)/shard_map/ppermute | solution.py:208
  412.1 39.4 %collective-permute-start.30 = (bf16[512,1024]{1,0:T(8,128)(2,1)}, bf16[512,1024]{1,0:T(8,128)(2,1)}, u32[]{:S(2)}, u32[]{:S(2)}) collective-permute-start(bf16[512,1024]{1,0:T(8,128)(2,1)} %add_convert_fusion.4), channel_id=1, source_target_pairs={{0,4},{4,8},{8,12},{12,14},{14,10},{10,6},{6,2},{2,0},{1,5},{5,9},... | collective-permute-start | bytes 3145736 | tf_op jit(solution)/shard_map/ppermute | solution.py:208
  417.5 34.1 %collective-permute-start.34 = (bf16[512,1024]{1,0:T(8,128)(2,1)}, bf16[512,1024]{1,0:T(8,128)(2,1)}, u32[]{:S(2)}, u32[]{:S(2)}) collective-permute-start(bf16[512,1024]{1,0:T(8,128)(2,1)} %add_convert_fusion.1), channel_id=1, source_target_pairs={{4,0},{8,4},{12,8},{14,12},{10,14},{6,10},{2,6},{0,2},{5,1},{9,5},... | collective-permute-start | bytes 3145736 | tf_op jit(solution)/shard_map/ppermute | solution.py:208
  (21 other events, 236.6 us)
